TPU v7x, 256 devices: a whole 4x4x8 slice. The times are simulated.
256 devices in a mesh: gx: 32 (over z_lo, x, core), gy: 8 (over z_hi, y).
Axes of the slice: x: 4, y: 4, z: 8 (z_hi: 2, z_lo: 4; z = z_hi * 4 + z_lo), core: 2. Of those that a mesh axis runs over, the one named last changes fastest.
Arguments:
- fields: float32 [3, 8, 768, 3072], P(None, None, 'gx', 'gy'), may hold values from -6 to 6
- east_band: float32 [2, 3, 8, 2, 1024], P(None, None, None, None, 'gy'), may hold values from -6 to 6
- north_band: float32 [2, 3, 8, 2, 256], P(None, None, None, None, 'gx'), may hold values from -6 to 6
- east_index: int32 [2, 3072], P(None, 'gy'), may hold values from 0 to 1022, as said below
- north_index: int32 [2, 768], P(None, 'gx'), may hold values from 0 to 254, as said below
- east_weight: float32 [2, 3072], P(None, 'gy'), may hold values from 0.15 to 0.85
- north_weight: float32 [2, 768], P(None, 'gx'), may hold values from 0.15 to 0.85
- nest_moves: int32 [2, 2], replicated, may hold values from -1 to 1, as said below
- courant: float32 [8], replicated, may hold values from 0.15 to 0.6
- diffuse: float32 [8], replicated, may hold values from 0.02 to 0.12
Outputs:
- advanced: float32 [3, 8, 768, 3072], P(None, None, 'gx', 'gy')
Inputs may be any that keep to these rules, and one draw needn't show every extreme that they name: `nest_moves`: each offset is -1 or 1, and the second move is the first reversed in both components. `east_index`: for each side, the donor row of nest row y is y//3 - 1 or y//3, clamped to 0 and 1022. `north_index`: for each side, the donor column of nest column x is x//3 - 1 or x//3, clamped to 0 and 254.
All inputs are finite; a program needn't handle non-finite values.
Results may differ from a plain program's by a relative error of at most 0.000096.
Values sent between devices are 32-bit elements; how exact they have to be, the bound alone decides.
A program may use at most 64 MiB of HBM per device.

v0:
```python
import jax
import jax.numpy as jnp
from jax import lax
from jax.sharding import PartitionSpec as P


def padded_2(cells, sides, width):
    for axis, dim in sides:
        count = lax.axis_size(axis)
        ends = count - 1
        head = lax.slice_in_dim(cells, 0, width, axis=dim)
        tail = lax.slice_in_dim(cells, cells.shape[dim] - width, cells.shape[dim], axis=dim)
        cells = jnp.concatenate(
            [
                lax.ppermute(tail, axis, [(i, (i + 1) % count) for i in range(ends)]),
                cells,
                lax.ppermute(head, axis, [((i + 1) % count, i) for i in range(ends)]),
            ],
            axis=dim,
        )
    return cells


def outward_weights(direction):
    places = jnp.arange(3).astype(jnp.float32)
    return jnp.where(direction > 0, (2.0 * places + 1.0) / 6.0, (5.0 - 2.0 * places) / 6.0)


def edge_values(banded, index_row, weight_row, direction, offset):
    outward = outward_weights(direction)
    blended = (
        banded[:, :, 0, None, :] * (1.0 - outward)[None, None, :, None]
        + banded[:, :, 1, None, :] * outward[None, None, :, None]
    )
    donor_count = banded.shape[3]
    where_low = index_row - offset + 2
    donors = jnp.arange(donor_count, dtype=jnp.int32)[:, None]
    matrix = jnp.where(donors == where_low[None, :], 1.0 - weight_row[None, :], 0.0) + jnp.where(
        donors == where_low[None, :] + 1, weight_row[None, :], 0.0
    )
    flattened = blended.reshape(-1, donor_count)
    result = jnp.dot(
        flattened, matrix, precision=lax.Precision.HIGHEST, preferred_element_type=jnp.float32
    )
    return result.reshape(blended.shape[0], blended.shape[1], 3, index_row.shape[0])


def place_strips(
    extended,
    margin,
    shift_east,
    shift_north,
    band_rows,
    band_cols,
    east_index,
    north_index,
    east_weight,
    north_weight,
    cells_east,
    cells_north,
):
    span_east = cells_east + 2 * margin
    span_north = cells_north + 2 * margin
    anchor = jnp.zeros((), jnp.int32)
    start_east = 3 + 3 * shift_east
    start_north = 3 + 3 * shift_north
    shifted = lax.dynamic_slice(
        extended,
        (anchor, anchor, start_east, start_north),
        (extended.shape[0], extended.shape[1], span_east, span_north),
    )
    global_east = (
        lax.axis_index("gx") * cells_east - margin + jnp.arange(span_east, dtype=jnp.int32)
    )
    global_north = (
        lax.axis_index("gy") * cells_north - margin + jnp.arange(span_north, dtype=jnp.int32)
    )
    total_east = cells_east * lax.axis_size("gx")
    total_north = cells_north * lax.axis_size("gy")
    side_east = (shift_east + 1) // 2
    offset_east = lax.axis_index("gy") * (cells_north // 3)
    strip_east = edge_values(
        lax.dynamic_index_in_dim(band_rows, side_east, 0, keepdims=False),
        lax.dynamic_index_in_dim(east_index, side_east, 0, keepdims=False),
        lax.dynamic_index_in_dim(east_weight, side_east, 0, keepdims=False),
        shift_east,
        offset_east,
    )
    first_east = jnp.where(shift_east > 0, total_east - 3, 0).astype(jnp.int32)
    for place in range(3):
        hit = global_east == first_east + place
        shifted = jnp.where(hit[None, None, :, None], strip_east[:, :, place, None, :], shifted)
    side_north = (shift_north + 1) // 2
    offset_north = lax.axis_index("gx") * (cells_east // 3)
    strip_north = edge_values(
        lax.dynamic_index_in_dim(band_cols, side_north, 0, keepdims=False),
        lax.dynamic_index_in_dim(north_index, side_north, 0, keepdims=False),
        lax.dynamic_index_in_dim(north_weight, side_north, 0, keepdims=False),
        shift_north,
        offset_north,
    )
    first_north = jnp.where(shift_north > 0, total_north - 3, 0).astype(jnp.int32)
    for place in range(3):
        hit = global_north == first_north + place
        shifted = jnp.where(hit[None, None, None, :], strip_north[:, :, place, :, None], shifted)
    inside = ((global_east >= 0) & (global_east < total_east))[:, None] & (
        (global_north >= 0) & (global_north < total_north)
    )[None, :]
    return jnp.where(inside[None, None], shifted, 0.0)


def laplace(padded, center):
    return (
        padded[:, 2:, 1:-1]
        + padded[:, :-2, 1:-1]
        + padded[:, 1:-1, 2:]
        + padded[:, 1:-1, :-2]
        - 4.0 * center
    )


def finish(pressure, zonal_pad, merid_pad, courant_col, viscous):
    zonal_mid = zonal_pad[:, 1:-1, 1:-1]
    merid_mid = merid_pad[:, 1:-1, 1:-1]
    zonal_new = zonal_mid + viscous * laplace(zonal_pad, zonal_mid)
    merid_new = merid_mid + viscous * laplace(merid_pad, merid_mid)
    pressure_new = pressure - 0.5 * courant_col * (
        zonal_pad[:, 2:, 1:-1]
        - zonal_pad[:, :-2, 1:-1]
        + (merid_pad[:, 1:-1, 2:] - merid_pad[:, 1:-1, :-2])
    )
    return jnp.stack([pressure_new, zonal_new, merid_new])


def body(
    fields,
    east_band,
    north_band,
    east_index,
    north_index,
    east_weight,
    north_weight,
    nest_moves,
    courant,
    diffuse,
):
    cells_east = fields.shape[2]
    cells_north = fields.shape[3]
    band_rows = padded_2(east_band, (("gy", 4),), 2)
    band_cols = padded_2(north_band, (("gx", 4),), 2)
    current = fields
    courant_col = courant[:, None, None]
    viscous = diffuse[:, None, None]
    for number in range(2):
        extended = padded_2(current, (("gx", 2), ("gy", 3)), 3)
        moved = place_strips(
            extended,
            0,
            nest_moves[number, 0],
            nest_moves[number, 1],
            band_rows,
            band_cols,
            east_index,
            north_index,
            east_weight,
            north_weight,
            cells_east,
            cells_north,
        )
        pressure = moved[0]
        padded = padded_2(pressure, (("gx", 1), ("gy", 2)), 1)
        zonal_first = moved[1] - 0.5 * courant_col * (padded[:, 2:, 1:-1] - padded[:, :-2, 1:-1])
        merid_first = moved[2] - 0.5 * courant_col * (padded[:, 1:-1, 2:] - padded[:, 1:-1, :-2])
        wind_halo = padded_2(jnp.stack([zonal_first, merid_first]), (("gx", 2), ("gy", 3)), 1)
        current = finish(pressure, wind_halo[0], wind_halo[1], courant_col, viscous)
    return current


def solution(mesh):
    return jax.shard_map(
        body,
        mesh=mesh,
        in_specs=(
            P(None, None, "gx", "gy"),
            P(None, None, None, None, "gy"),
            P(None, None, None, None, "gx"),
            P(None, "gy"),
            P(None, "gx"),
            P(None, "gy"),
            P(None, "gx"),
            P(),
            P(),
            P(),
        ),
        out_specs=P(None, None, "gx", "gy"),
        check_vma=False,
    )
```

profile of v0, /device:TPU:95, one launch (start us, length us, event | category | flops | bytes accessed | tf_op | source)
XLA Modules:
  0.0 243.2 jit_solution(5449530573557481535)
XLA Ops:
  1.1 4.0 %collective-permute-start = (f32[2,3,8,2,2]{4,3,2,1,0:T(2,128)S(1)}, f32[2,3,8,2,2]{4,3,2,1,0:T(2,128)S(1)}, u32[]{:S(2)}, u32[]{:S(2)}) collective-permute-start(f32[2,3,8,2,2]{4,3,2,1,0:T(2,128)S(1)} %get-tuple-element.63), channel_id=1, source_target_pairs={{0,8},{8,16},{16,24},{24,32},{32,40},{40,48},{48,56},{56,64},{64,7... | collective-permute-start | bytes 2312 | tf_op jit(solution)/shard_map/ppermute | solution.py:15
  8.0 5.8 %collective-permute-start.2 = (f32[2,3,8,2,2]{4,3,2,1,0:T(2,128)S(1)}, f32[2,3,8,2,2]{4,3,2,1,0:T(2,128)S(1)}, u32[]{:S(2)}, u32[]{:S(2)}) collective-permute-start(f32[2,3,8,2,2]{4,3,2,1,0:T(2,128)S(1)} %get-tuple-element.67), channel_id=1, source_target_pairs={{0,1},{1,2},{2,3},{3,4},{4,5},{5,6},{6,7},{8,9},{9,10},{10,11},{11... | collective-permute-start | bytes 2312 | tf_op jit(solution)/shard_map/ppermute | solution.py:15
  16.8 6.0 %collective-permute-start.4 = (f32[3,8,3,384]{3,2,1,0:T(4,128)S(1)}, f32[3,8,3,384]{3,2,1,0:T(4,128)S(1)}, u32[]{:S(2)}, u32[]{:S(2)}) collective-permute-start(f32[3,8,3,384]{3,2,1,0:T(4,128)S(1)} %get-tuple-element.27), channel_id=1, source_target_pairs={{0,8},{8,16},{16,24},{24,32},{32,40},{40,48},{48,56},{56,64},{64,7... | collective-permute-start | bytes 331784 | tf_op jit(solution)/shard_map/ppermute | solution.py:15
  34.7 5.3 %collective-permute-done.5 = f32[3,8,3,384]{3,2,1,0:T(4,128)S(1)} collective-permute-done((f32[3,8,3,384]{3,2,1,0:T(4,128)S(1)}, f32[3,8,3,384]{3,2,1,0:T(4,128)S(1)}, u32[]{:S(2)}, u32[]{:S(2)}) %collective-permute-start.5) | collective-permute-done | bytes 110624 | tf_op jit(solution)/shard_map/ppermute | solution.py:17
  40.3 9.7 %collective-permute-start.6 = (f32[3,8,30,3]{3,2,1,0:T(8,128)S(1)}, f32[3,8,30,3]{3,2,1,0:T(8,128)S(1)}, u32[]{:S(2)}, u32[]{:S(2)}) collective-permute-start(f32[3,8,30,3]{3,2,1,0:T(8,128)S(1)} %get-tuple-element.20), channel_id=1, source_target_pairs={{0,1},{1,2},{2,3},{3,4},{4,5},{5,6},{6,7},{8,9},{9,10},{10,11},{11... | collective-permute-start | bytes 25928 | tf_op jit(solution)/shard_map/ppermute | solution.py:15
  51.9 11.0 %collective-permute-done.6 = f32[3,8,30,3]{3,2,1,0:T(8,128)S(1)} collective-permute-done((f32[3,8,30,3]{3,2,1,0:T(8,128)S(1)}, f32[3,8,30,3]{3,2,1,0:T(8,128)S(1)}, u32[]{:S(2)}, u32[]{:S(2)}) %collective-permute-start.6) | collective-permute-done | bytes 8672 | tf_op jit(solution)/shard_map/ppermute | solution.py:15
  62.9 10.1 %collective-permute-done.7 = f32[3,8,30,3]{3,2,1,0:T(8,128)S(1)} collective-permute-done((f32[3,8,30,3]{3,2,1,0:T(8,128)S(1)}, f32[3,8,30,3]{3,2,1,0:T(8,128)S(1)}, u32[]{:S(2)}, u32[]{:S(2)}) %collective-permute-start.7) | collective-permute-done | bytes 8672 | tf_op jit(solution)/shard_map/ppermute | solution.py:17
  76.5 5.8 %collective-permute-start.9 = (f32[8,1,384]{2,1,0:T(1,128)S(1)}, f32[8,1,384]{2,1,0:T(1,128)S(1)}, u32[]{:S(2)}, u32[]{:S(2)}) collective-permute-start(f32[8,1,384]{2,1,0:T(1,128)S(1)} %get-tuple-element.49), channel_id=1, source_target_pairs={{0,8},{8,16},{16,24},{24,32},{32,40},{40,48},{48,56},{56,64},{64,7... | collective-permute-start | bytes 36872 | tf_op jit(solution)/shard_map/ppermute | solution.py:15
  85.1 9.4 %collective-permute-start.11 = (f32[8,26,1]{2,1,0:T(8,128)S(1)}, f32[8,26,1]{2,1,0:T(8,128)S(1)}, u32[]{:S(2)}, u32[]{:S(2)}) collective-permute-start(f32[8,26,1]{2,1,0:T(8,128)S(1)} %get-tuple-element.46), channel_id=1, source_target_pairs={{0,1},{1,2},{2,3},{3,4},{4,5},{5,6},{6,7},{8,9},{9,10},{10,11},{11... | collective-permute-start | bytes 2504 | tf_op jit(solution)/shard_map/ppermute | solution.py:15
  98.3 5.9 %collective-permute-start.12 = (f32[2,8,1,384]{3,2,1,0:T(1,128)S(1)}, f32[2,8,1,384]{3,2,1,0:T(1,128)S(1)}, u32[]{:S(2)}, u32[]{:S(2)}) collective-permute-start(f32[2,8,1,384]{3,2,1,0:T(1,128)S(1)} %get-tuple-element.35), channel_id=1, source_target_pairs={{0,8},{8,16},{16,24},{24,32},{32,40},{40,48},{48,56},{56,64},{64,7... | collective-permute-start | bytes 73736 | tf_op jit(solution)/shard_map/ppermute | solution.py:15
  106.6 5.0 %collective-permute-done.13 = f32[2,8,1,384]{3,2,1,0:T(1,128)S(1)} collective-permute-done((f32[2,8,1,384]{3,2,1,0:T(1,128)S(1)}, f32[2,8,1,384]{3,2,1,0:T(1,128)S(1)}, u32[]{:S(2)}, u32[]{:S(2)}) %collective-permute-start.13) | collective-permute-done | bytes 24608 | tf_op jit(solution)/shard_map/ppermute | solution.py:17
  111.7 10.1 %collective-permute-start.14 = (f32[2,8,26,1]{3,2,1,0:T(8,128)S(1)}, f32[2,8,26,1]{3,2,1,0:T(8,128)S(1)}, u32[]{:S(2)}, u32[]{:S(2)}) collective-permute-start(f32[2,8,26,1]{3,2,1,0:T(8,128)S(1)} %get-tuple-element.31), channel_id=1, source_target_pairs={{0,1},{1,2},{2,3},{3,4},{4,5},{5,6},{6,7},{8,9},{9,10},{10,11},{11... | collective-permute-start | bytes 5000 | tf_op jit(solution)/shard_map/ppermute | solution.py:15
  123.7 4.9 %collective-permute-done.14 = f32[2,8,26,1]{3,2,1,0:T(8,128)S(1)} collective-permute-done((f32[2,8,26,1]{3,2,1,0:T(8,128)S(1)}, f32[2,8,26,1]{3,2,1,0:T(8,128)S(1)}, u32[]{:S(2)}, u32[]{:S(2)}) %collective-permute-start.14) | collective-permute-done | bytes 1696 | tf_op jit(solution)/shard_map/ppermute | solution.py:15
  128.6 10.1 %collective-permute-done.15 = f32[2,8,26,1]{3,2,1,0:T(8,128)S(1)} collective-permute-done((f32[2,8,26,1]{3,2,1,0:T(8,128)S(1)}, f32[2,8,26,1]{3,2,1,0:T(8,128)S(1)}, u32[]{:S(2)}, u32[]{:S(2)}) %collective-permute-start.15) | collective-permute-done | bytes 1696 | tf_op jit(solution)/shard_map/ppermute | solution.py:17
  145.4 7.0 %collective-permute-done.17 = f32[3,8,3,384]{3,2,1,0:T(4,128)S(1)} collective-permute-done((f32[3,8,3,384]{3,2,1,0:T(4,128)S(1)}, f32[3,8,3,384]{3,2,1,0:T(4,128)S(1)}, u32[]{:S(2)}, u32[]{:S(2)}) %collective-permute-start.17) | collective-permute-done | bytes 110624 | tf_op jit(solution)/shard_map/ppermute | solution.py:17
  157.9 7.9 %collective-permute-done.18 = f32[3,8,30,3]{3,2,1,0:T(8,128)S(1)} collective-permute-done((f32[3,8,30,3]{3,2,1,0:T(8,128)S(1)}, f32[3,8,30,3]{3,2,1,0:T(8,128)S(1)}, u32[]{:S(2)}, u32[]{:S(2)}) %collective-permute-start.18) | collective-permute-done | bytes 8672 | tf_op jit(solution)/shard_map/ppermute | solution.py:15
  165.8 10.1 %collective-permute-done.19 = f32[3,8,30,3]{3,2,1,0:T(8,128)S(1)} collective-permute-done((f32[3,8,30,3]{3,2,1,0:T(8,128)S(1)}, f32[3,8,30,3]{3,2,1,0:T(8,128)S(1)}, u32[]{:S(2)}, u32[]{:S(2)}) %collective-permute-start.19) | collective-permute-done | bytes 8672 | tf_op jit(solution)/shard_map/ppermute | solution.py:17
  179.5 5.8 %collective-permute-start.21 = (f32[8,1,384]{2,1,0:T(1,128)S(1)}, f32[8,1,384]{2,1,0:T(1,128)S(1)}, u32[]{:S(2)}, u32[]{:S(2)}) collective-permute-start(f32[8,1,384]{2,1,0:T(1,128)S(1)} %get-tuple-element.47), channel_id=1, source_target_pairs={{0,8},{8,16},{16,24},{24,32},{32,40},{40,48},{48,56},{56,64},{64,7... | collective-permute-start | bytes 36872 | tf_op jit(solution)/shard_map/ppermute | solution.py:15
  188.1 9.4 %collective-permute-start.23 = (f32[8,26,1]{2,1,0:T(8,128)S(1)}, f32[8,26,1]{2,1,0:T(8,128)S(1)}, u32[]{:S(2)}, u32[]{:S(2)}) collective-permute-start(f32[8,26,1]{2,1,0:T(8,128)S(1)} %get-tuple-element.44), channel_id=1, source_target_pairs={{0,1},{1,2},{2,3},{3,4},{4,5},{5,6},{6,7},{8,9},{9,10},{10,11},{11... | collective-permute-start | bytes 2504 | tf_op jit(solution)/shard_map/ppermute | solution.py:15
  199.8 7.4 %collective-permute-start.24 = (f32[2,8,1,384]{3,2,1,0:T(1,128)S(1)}, f32[2,8,1,384]{3,2,1,0:T(1,128)S(1)}, u32[]{:S(2)}, u32[]{:S(2)}) collective-permute-start(f32[2,8,1,384]{3,2,1,0:T(1,128)S(1)} %get-tuple-element.33), channel_id=1, source_target_pairs={{0,8},{8,16},{16,24},{24,32},{32,40},{40,48},{48,56},{56,64},{64,7... | collective-permute-start | bytes 73736 | tf_op jit(solution)/shard_map/ppermute | solution.py:15
  209.2 5.3 %collective-permute-done.25 = f32[2,8,1,384]{3,2,1,0:T(1,128)S(1)} collective-permute-done((f32[2,8,1,384]{3,2,1,0:T(1,128)S(1)}, f32[2,8,1,384]{3,2,1,0:T(1,128)S(1)}, u32[]{:S(2)}, u32[]{:S(2)}) %collective-permute-start.25) | collective-permute-done | bytes 24608 | tf_op jit(solution)/shard_map/ppermute | solution.py:17
  214.7 10.1 %collective-permute-start.26 = (f32[2,8,26,1]{3,2,1,0:T(8,128)S(1)}, f32[2,8,26,1]{3,2,1,0:T(8,128)S(1)}, u32[]{:S(2)}, u32[]{:S(2)}) collective-permute-start(f32[2,8,26,1]{3,2,1,0:T(8,128)S(1)} %get-tuple-element.29), channel_id=1, source_target_pairs={{0,1},{1,2},{2,3},{3,4},{4,5},{5,6},{6,7},{8,9},{9,10},{10,11},{11... | collective-permute-start | bytes 5000 | tf_op jit(solution)/shard_map/ppermute | solution.py:15
  226.7 4.0 %collective-permute-done.26 = f32[2,8,26,1]{3,2,1,0:T(8,128)S(1)} collective-permute-done((f32[2,8,26,1]{3,2,1,0:T(8,128)S(1)}, f32[2,8,26,1]{3,2,1,0:T(8,128)S(1)}, u32[]{:S(2)}, u32[]{:S(2)}) %collective-permute-start.26) | collective-permute-done | bytes 1696 | tf_op jit(solution)/shard_map/ppermute | solution.py:15
  230.7 10.1 %collective-permute-done.27 = f32[2,8,26,1]{3,2,1,0:T(8,128)S(1)} collective-permute-done((f32[2,8,26,1]{3,2,1,0:T(8,128)S(1)}, f32[2,8,26,1]{3,2,1,0:T(8,128)S(1)}, u32[]{:S(2)}, u32[]{:S(2)}) %collective-permute-start.27) | collective-permute-done | bytes 1696 | tf_op jit(solution)/shard_map/ppermute | solution.py:17
  (114 shorter events, 54.3 us)
Async XLA Ops:
  1.1 30.4 %collective-permute-start = (f32[2,3,8,2,2]{4,3,2,1,0:T(2,128)S(1)}, f32[2,3,8,2,2]{4,3,2,1,0:T(2,128)S(1)}, u32[]{:S(2)}, u32[]{:S(2)}) collective-permute-start(f32[2,3,8,2,2]{4,3,2,1,0:T(2,128)S(1)} %get-tuple-element.63), channel_id=1, source_target_pairs={{0,8},{8,16},{16,24},{24,32},{32,40},{40,48},{48,56},{56,64},{64,7... | collective-permute-start | bytes 2312 | tf_op jit(solution)/shard_map/ppermute | solution.py:15
  5.1 28.4 %collective-permute-start.1 = (f32[2,3,8,2,2]{4,3,2,1,0:T(2,128)S(1)}, f32[2,3,8,2,2]{4,3,2,1,0:T(2,128)S(1)}, u32[]{:S(2)}, u32[]{:S(2)}) collective-permute-start(f32[2,3,8,2,2]{4,3,2,1,0:T(2,128)S(1)} %get-tuple-element.64), channel_id=1, source_target_pairs={{8,0},{16,8},{24,16},{32,24},{40,32},{48,40},{56,48},{64,56},{72,6... | collective-permute-start | bytes 2312 | tf_op jit(solution)/shard_map/ppermute | solution.py:17
  8.0 25.7 %collective-permute-start.2 = (f32[2,3,8,2,2]{4,3,2,1,0:T(2,128)S(1)}, f32[2,3,8,2,2]{4,3,2,1,0:T(2,128)S(1)}, u32[]{:S(2)}, u32[]{:S(2)}) collective-permute-start(f32[2,3,8,2,2]{4,3,2,1,0:T(2,128)S(1)} %get-tuple-element.67), channel_id=1, source_target_pairs={{0,1},{1,2},{2,3},{3,4},{4,5},{5,6},{6,7},{8,9},{9,10},{10,11},{11... | collective-permute-start | bytes 2312 | tf_op jit(solution)/shard_map/ppermute | solution.py:15
  13.8 19.9 %collective-permute-start.3 = (f32[2,3,8,2,2]{4,3,2,1,0:T(2,128)S(1)}, f32[2,3,8,2,2]{4,3,2,1,0:T(2,128)S(1)}, u32[]{:S(2)}, u32[]{:S(2)}) collective-permute-start(f32[2,3,8,2,2]{4,3,2,1,0:T(2,128)S(1)} %get-tuple-element.68), channel_id=1, source_target_pairs={{1,0},{2,1},{3,2},{4,3},{5,4},{6,5},{7,6},{9,8},{10,9},{11,10},{12... | collective-permute-start | bytes 2312 | tf_op jit(solution)/shard_map/ppermute | solution.py:17
  16.8 17.9 %collective-permute-start.4 = (f32[3,8,3,384]{3,2,1,0:T(4,128)S(1)}, f32[3,8,3,384]{3,2,1,0:T(4,128)S(1)}, u32[]{:S(2)}, u32[]{:S(2)}) collective-permute-start(f32[3,8,3,384]{3,2,1,0:T(4,128)S(1)} %get-tuple-element.27), channel_id=1, source_target_pairs={{0,8},{8,16},{16,24},{24,32},{32,40},{40,48},{48,56},{56,64},{64,7... | collective-permute-start | bytes 331784 | tf_op jit(solution)/shard_map/ppermute | solution.py:15
  31.5 8.6 %collective-permute-start.5 = (f32[3,8,3,384]{3,2,1,0:T(4,128)S(1)}, f32[3,8,3,384]{3,2,1,0:T(4,128)S(1)}, u32[]{:S(2)}, u32[]{:S(2)}) collective-permute-start(f32[3,8,3,384]{3,2,1,0:T(4,128)S(1)} %get-tuple-element.28), channel_id=1, source_target_pairs={{8,0},{16,8},{24,16},{32,24},{40,32},{48,40},{56,48},{64,56},{72,6... | collective-permute-start | bytes 331784 | tf_op jit(solution)/shard_map/ppermute | solution.py:17
  40.3 22.6 %collective-permute-start.6 = (f32[3,8,30,3]{3,2,1,0:T(8,128)S(1)}, f32[3,8,30,3]{3,2,1,0:T(8,128)S(1)}, u32[]{:S(2)}, u32[]{:S(2)}) collective-permute-start(f32[3,8,30,3]{3,2,1,0:T(8,128)S(1)} %get-tuple-element.20), channel_id=1, source_target_pairs={{0,1},{1,2},{2,3},{3,4},{4,5},{5,6},{6,7},{8,9},{9,10},{10,11},{11... | collective-permute-start | bytes 25928 | tf_op jit(solution)/shard_map/ppermute | solution.py:15
  50.0 23.0 %collective-permute-start.7 = (f32[3,8,30,3]{3,2,1,0:T(8,128)S(1)}, f32[3,8,30,3]{3,2,1,0:T(8,128)S(1)}, u32[]{:S(2)}, u32[]{:S(2)}) collective-permute-start(f32[3,8,30,3]{3,2,1,0:T(8,128)S(1)} %get-tuple-element.19), channel_id=1, source_target_pairs={{1,0},{2,1},{3,2},{4,3},{5,4},{6,5},{7,6},{9,8},{10,9},{11,10},{12... | collective-permute-start | bytes 25928 | tf_op jit(solution)/shard_map/ppermute | solution.py:17
  74.6 8.3 %collective-permute-start.8 = (f32[8,1,384]{2,1,0:T(1,128)S(1)}, f32[8,1,384]{2,1,0:T(1,128)S(1)}, u32[]{:S(2)}, u32[]{:S(2)}) collective-permute-start(f32[8,1,384]{2,1,0:T(1,128)S(1)} %get-tuple-element.50), channel_id=1, source_target_pairs={{8,0},{16,8},{24,16},{32,24},{40,32},{48,40},{56,48},{64,56},{72,6... | collective-permute-start | bytes 36872 | tf_op jit(solution)/shard_map/ppermute | solution.py:17
  83.2 13.6 %collective-permute-start.10 = (f32[8,26,1]{2,1,0:T(8,128)S(1)}, f32[8,26,1]{2,1,0:T(8,128)S(1)}, u32[]{:S(2)}, u32[]{:S(2)}) collective-permute-start(f32[8,26,1]{2,1,0:T(8,128)S(1)} %get-tuple-element.45), channel_id=1, source_target_pairs={{1,0},{2,1},{3,2},{4,3},{5,4},{6,5},{7,6},{9,8},{10,9},{11,10},{12... | collective-permute-start | bytes 2504 | tf_op jit(solution)/shard_map/ppermute | solution.py:17
  85.1 12.8 %collective-permute-start.11 = (f32[8,26,1]{2,1,0:T(8,128)S(1)}, f32[8,26,1]{2,1,0:T(8,128)S(1)}, u32[]{:S(2)}, u32[]{:S(2)}) collective-permute-start(f32[8,26,1]{2,1,0:T(8,128)S(1)} %get-tuple-element.46), channel_id=1, source_target_pairs={{0,1},{1,2},{2,3},{3,4},{4,5},{5,6},{6,7},{8,9},{9,10},{10,11},{11... | collective-permute-start | bytes 2504 | tf_op jit(solution)/shard_map/ppermute | solution.py:15
  98.3 8.2 %collective-permute-start.12 = (f32[2,8,1,384]{3,2,1,0:T(1,128)S(1)}, f32[2,8,1,384]{3,2,1,0:T(1,128)S(1)}, u32[]{:S(2)}, u32[]{:S(2)}) collective-permute-start(f32[2,8,1,384]{3,2,1,0:T(1,128)S(1)} %get-tuple-element.35), channel_id=1, source_target_pairs={{0,8},{8,16},{16,24},{24,32},{32,40},{40,48},{48,56},{56,64},{64,7... | collective-permute-start | bytes 73736 | tf_op jit(solution)/shard_map/ppermute | solution.py:15
  104.3 7.3 %collective-permute-start.13 = (f32[2,8,1,384]{3,2,1,0:T(1,128)S(1)}, f32[2,8,1,384]{3,2,1,0:T(1,128)S(1)}, u32[]{:S(2)}, u32[]{:S(2)}) collective-permute-start(f32[2,8,1,384]{3,2,1,0:T(1,128)S(1)} %get-tuple-element.36), channel_id=1, source_target_pairs={{8,0},{16,8},{24,16},{32,24},{40,32},{48,40},{56,48},{64,56},{72,6... | collective-permute-start | bytes 73736 | tf_op jit(solution)/shard_map/ppermute | solution.py:17
  111.7 16.9 %collective-permute-start.14 = (f32[2,8,26,1]{3,2,1,0:T(8,128)S(1)}, f32[2,8,26,1]{3,2,1,0:T(8,128)S(1)}, u32[]{:S(2)}, u32[]{:S(2)}) collective-permute-start(f32[2,8,26,1]{3,2,1,0:T(8,128)S(1)} %get-tuple-element.31), channel_id=1, source_target_pairs={{0,1},{1,2},{2,3},{3,4},{4,5},{5,6},{6,7},{8,9},{9,10},{10,11},{11... | collective-permute-start | bytes 5000 | tf_op jit(solution)/shard_map/ppermute | solution.py:15
  121.8 16.9 %collective-permute-start.15 = (f32[2,8,26,1]{3,2,1,0:T(8,128)S(1)}, f32[2,8,26,1]{3,2,1,0:T(8,128)S(1)}, u32[]{:S(2)}, u32[]{:S(2)}) collective-permute-start(f32[2,8,26,1]{3,2,1,0:T(8,128)S(1)} %get-tuple-element.32), channel_id=1, source_target_pairs={{1,0},{2,1},{3,2},{4,3},{5,4},{6,5},{7,6},{9,8},{10,9},{11,10},{12... | collective-permute-start | bytes 5000 | tf_op jit(solution)/shard_map/ppermute | solution.py:17
  142.7 9.7 %collective-permute-start.17 = (f32[3,8,3,384]{3,2,1,0:T(4,128)S(1)}, f32[3,8,3,384]{3,2,1,0:T(4,128)S(1)}, u32[]{:S(2)}, u32[]{:S(2)}) collective-permute-start(f32[3,8,3,384]{3,2,1,0:T(4,128)S(1)} %get-tuple-element.26), channel_id=1, source_target_pairs={{8,0},{16,8},{24,16},{32,24},{40,32},{48,40},{56,48},{64,56},{72,6... | collective-permute-start | bytes 331784 | tf_op jit(solution)/shard_map/ppermute | solution.py:17
  152.6 13.2 %collective-permute-start.18 = (f32[3,8,30,3]{3,2,1,0:T(8,128)S(1)}, f32[3,8,30,3]{3,2,1,0:T(8,128)S(1)}, u32[]{:S(2)}, u32[]{:S(2)}) collective-permute-start(f32[3,8,30,3]{3,2,1,0:T(8,128)S(1)} %get-tuple-element.18), channel_id=1, source_target_pairs={{0,1},{1,2},{2,3},{3,4},{4,5},{5,6},{6,7},{8,9},{9,10},{10,11},{11... | collective-permute-start | bytes 25928 | tf_op jit(solution)/shard_map/ppermute | solution.py:15
  154.5 21.4 %collective-permute-start.19 = (f32[3,8,30,3]{3,2,1,0:T(8,128)S(1)}, f32[3,8,30,3]{3,2,1,0:T(8,128)S(1)}, u32[]{:S(2)}, u32[]{:S(2)}) collective-permute-start(f32[3,8,30,3]{3,2,1,0:T(8,128)S(1)} %get-tuple-element.17), channel_id=1, source_target_pairs={{1,0},{2,1},{3,2},{4,3},{5,4},{6,5},{7,6},{9,8},{10,9},{11,10},{12... | collective-permute-start | bytes 25928 | tf_op jit(solution)/shard_map/ppermute | solution.py:17
  177.6 7.7 %collective-permute-start.20 = (f32[8,1,384]{2,1,0:T(1,128)S(1)}, f32[8,1,384]{2,1,0:T(1,128)S(1)}, u32[]{:S(2)}, u32[]{:S(2)}) collective-permute-start(f32[8,1,384]{2,1,0:T(1,128)S(1)} %get-tuple-element.48), channel_id=1, source_target_pairs={{8,0},{16,8},{24,16},{32,24},{40,32},{48,40},{56,48},{64,56},{72,6... | collective-permute-start | bytes 36872 | tf_op jit(solution)/shard_map/ppermute | solution.py:17
  186.2 11.7 %collective-permute-start.22 = (f32[8,26,1]{2,1,0:T(8,128)S(1)}, f32[8,26,1]{2,1,0:T(8,128)S(1)}, u32[]{:S(2)}, u32[]{:S(2)}) collective-permute-start(f32[8,26,1]{2,1,0:T(8,128)S(1)} %get-tuple-element.43), channel_id=1, source_target_pairs={{1,0},{2,1},{3,2},{4,3},{5,4},{6,5},{7,6},{9,8},{10,9},{11,10},{12... | collective-permute-start | bytes 2504 | tf_op jit(solution)/shard_map/ppermute | solution.py:17
  188.1 11.3 %collective-permute-start.23 = (f32[8,26,1]{2,1,0:T(8,128)S(1)}, f32[8,26,1]{2,1,0:T(8,128)S(1)}, u32[]{:S(2)}, u32[]{:S(2)}) collective-permute-start(f32[8,26,1]{2,1,0:T(8,128)S(1)} %get-tuple-element.44), channel_id=1, source_target_pairs={{0,1},{1,2},{2,3},{3,4},{4,5},{5,6},{6,7},{8,9},{9,10},{10,11},{11... | collective-permute-start | bytes 2504 | tf_op jit(solution)/shard_map/ppermute | solution.py:15
  199.8 9.4 %collective-permute-start.24 = (f32[2,8,1,384]{3,2,1,0:T(1,128)S(1)}, f32[2,8,1,384]{3,2,1,0:T(1,128)S(1)}, u32[]{:S(2)}, u32[]{:S(2)}) collective-permute-start(f32[2,8,1,384]{3,2,1,0:T(1,128)S(1)} %get-tuple-element.33), channel_id=1, source_target_pairs={{0,8},{8,16},{16,24},{24,32},{32,40},{40,48},{48,56},{56,64},{64,7... | collective-permute-start | bytes 73736 | tf_op jit(solution)/shard_map/ppermute | solution.py:15
  214.7 16.0 %collective-permute-start.26 = (f32[2,8,26,1]{3,2,1,0:T(8,128)S(1)}, f32[2,8,26,1]{3,2,1,0:T(8,128)S(1)}, u32[]{:S(2)}, u32[]{:S(2)}) collective-permute-start(f32[2,8,26,1]{3,2,1,0:T(8,128)S(1)} %get-tuple-element.29), channel_id=1, source_target_pairs={{0,1},{1,2},{2,3},{3,4},{4,5},{5,6},{6,7},{8,9},{9,10},{10,11},{11... | collective-permute-start | bytes 5000 | tf_op jit(solution)/shard_map/ppermute | solution.py:15
  224.8 16.1 %collective-permute-start.27 = (f32[2,8,26,1]{3,2,1,0:T(8,128)S(1)}, f32[2,8,26,1]{3,2,1,0:T(8,128)S(1)}, u32[]{:S(2)}, u32[]{:S(2)}) collective-permute-start(f32[2,8,26,1]{3,2,1,0:T(8,128)S(1)} %get-tuple-element.30), channel_id=1, source_target_pairs={{1,0},{2,1},{3,2},{4,3},{5,4},{6,5},{7,6},{9,8},{10,9},{11,10},{12... | collective-permute-start | bytes 5000 | tf_op jit(solution)/shard_map/ppermute | solution.py:17
  (13 other events, 263.0 us)
where the time goes:
time: 244 us; the launch traced here: 243 us
  starting transfers between devices  122 us (50%)
  waiting for transfers between devices  96.4 us (40%)
  other arithmetic  9.22 us (4%)
  between operations  8.81 us (4%)
  local copies, waits for them, and re-layouts  5.6 us (2%)
    ppermute x14, starting transfers between devices, padded_2(): lax.ppermute(tail, axis, [(i, (i + 1) % count) for i in range(ends)])  93.1 us
    ppermute x14, waiting for transfers between devices, padded_2(): lax.ppermute(head, axis, [((i + 1) % count, i) for i in range(ends)])  65 us
    ppermute x14, waiting for transfers between devices, padded_2(): lax.ppermute(tail, axis, [(i, (i + 1) % count) for i in range(ends)])  31.4 us
    ppermute x14, starting transfers between devices, padded_2(): lax.ppermute(head, axis, [((i + 1) % count, i) for i in range(ends)])  28.8 us
  transfers between devices with their start and end apart: 28, of which 18 were waited for; matrix products, arithmetic and copies ran while one was open for 2% of the time, Pallas kernels for 0%

commit v1 on v0

v1 whole, which is shorter than its diff:
```python
import functools

import jax
import jax.numpy as jnp
from jax import lax
from jax.experimental import pallas as pl
from jax.experimental.pallas import tpu as pltpu
from jax.sharding import PartitionSpec as P

MESH = pl.DeviceIdType.MESH
F32 = jnp.float32
I32 = jnp.int32
HALO = 4
ROWS = 24
SPAN = ROWS + 2 * HALO
WIDE = 384
LANES = 128
LEVELS = 8
X_ROWS = (4, 3, 2)


def third(v):
    return (((v + 48) * 43691) >> 17) - 16


def roll(v, by):
    size = v.shape[1]
    by = by % size
    return pltpu.roll(v, by, 1) if by else v


def iota():
    return lax.broadcasted_iota(I32, (LEVELS, LANES), 1)


def take(v, at):
    return jnp.take_along_axis(v, at & (LANES - 1), axis=1)


def pick_shift(v, by, step):
    return jnp.where(by > 0, roll(v, step), jnp.where(by < 0, roll(v, -step), v))


def edge_block(head, tail):
    lane = iota()
    return jnp.where((lane >= 32) & (lane < 64), roll(tail, 64), head)


def edge_cells():
    lane = iota()
    return jnp.where(lane < 32, lane, jnp.where(lane < 96, lane + (WIDE - 64), lane - LANES))


def slots():
    lane = iota()
    return jnp.where((lane & 7) < 4, ((lane + 64) & 127) >> 3, ((lane + 4) & 127) >> 3)


def advance(load, store, lo, hi, kk, kk_row, visc, unroll):
    def first(r, p_below, p_here, p_above):
        k = kk_row(r)
        u = load(1, r) - k * (p_above - p_below)
        v = load(2, r) - k * (roll(p_here, -1) - roll(p_here, 1))
        return u, v

    def row(r, carry):
        p0, p1, ub, u0, vb, v0 = carry
        p2 = load(0, r + 2)
        ua, va = first(r + 1, p0, p1, p2)
        un, us, vn, vs = roll(u0, -1), roll(u0, 1), roll(v0, -1), roll(v0, 1)
        store(0, r, p0 - kk * ((ua - ub) + (vn - vs)))
        store(1, r, u0 + visc * (((ua + ub) + (un + us)) - 4.0 * u0))
        store(2, r, v0 + visc * (((va + vb) + (vn + vs)) - 4.0 * v0))
        return p1, p2, u0, ua, v0, va

    p = [load(0, lo - 2 + i) for i in range(4)]
    ub, vb = first(lo - 1, p[0], p[1], p[2])
    u0, v0 = first(lo, p[1], p[2], p[3])
    carry = (p[2], p[3], ub, u0, vb, v0)
    if unroll is None:
        for r in range(lo, hi):
            carry = row(r, carry)
    else:
        lax.fori_loop(lo, hi, row, carry, unroll=unroll)


def exchange_kernel(
    sizes,
    fields,
    east_band,
    north_band,
    east_index,
    north_index,
    east_weight,
    north_weight,
    moves,
    courant,
    diffuse,
    out,
    ext,
    gxt,
    mid,
    midg,
    packed,
    from_y,
    from_d,
    east_out,
    east_in,
    north_out,
    north_in,
    strip,
    strip_g,
    ns,
    eb,
    ei,
    ew,
    nb,
    nbw,
    ni,
    nw,
    ntab,
    mv,
    ks,
    qs,
    in_sem,
    small_sem,
    x_send,
    x_recv,
    y_send,
    y_recv,
    d_send,
    d_recv,
    ea_send,
    ea_recv,
    na_send,
    na_recv,
):
    nx, ny = sizes
    gx = lax.axis_index("gx")
    gy = lax.axis_index("gy")
    total_x = nx * ROWS
    total_y = ny * WIDE
    west, east = gx == 0, gx == nx - 1
    south, north = gy == 0, gy == ny - 1
    x_edge = jnp.logical_or(west, east)
    y_edge = jnp.logical_or(south, north)
    has_x = {-1: gx > 0, 1: gx < nx - 1}
    has_y = {-1: gy > 0, 1: gy < ny - 1}

    def has(dx, dy):
        if dx and dy:
            return jnp.logical_and(has_x[dx], has_y[dy])
        return has_x[dx] if dx else has_y[dy]

    around = [(dx, dy) for dy in (-1, 1, 0) for dx in (-1, 0, 1) if dx or dy]
    barrier = pltpu.get_barrier_semaphore()
    for dx, dy in around:

        @pl.when(has(dx, dy))
        def _(dx=dx, dy=dy):
            pl.semaphore_signal(barrier, inc=1, device_id=(gx + dx, gy + dy), device_id_type=MESH)

    loads = [
        pltpu.make_async_copy(fields.at[f, l], ext.at[f, HALO : HALO + ROWS, l, :], in_sem.at[f * LEVELS + l])
        for f in range(3)
        for l in range(LEVELS)
    ]
    smalls = [
        pltpu.make_async_copy(s, d, small_sem.at[k])
        for k, (s, d) in enumerate(
            (
                (moves, mv),
                (courant, ks),
                (diffuse, qs),
                (east_band, eb),
                (east_index, ei),
                (east_weight, ew),
                (north_band, nb),
                (north_index, ni),
                (north_weight, nw),
            )
        )
    ]
    for c in loads + smalls:
        c.start()
    for c in loads:
        c.wait()

    lane = iota()
    slot = slots()
    keep = {}
    for r in range(HALO, HALO + ROWS):
        h, i = divmod(r, 16)
        for f in range(3):
            block = edge_block(ext[f, r, :, 0:LANES], ext[f, r, :, 2 * LANES : WIDE])
            gxt[f, r] = block
            moved = roll(block, 8 * i + 64)
            keep[h, f] = jnp.where(slot == i, moved, keep[h, f]) if (h, f) in keep else moved
    for (h, f), v in keep.items():
        packed[h, f] = v
    for c in smalls:
        c.wait()

    shift_x = mv[0, 0]
    shift_y = mv[0, 1]
    side_x = jnp.where(west, 0, 1)
    side_y = jnp.where(south, 0, 1)
    out_x = shift_x == 2 * side_x - 1
    out_y = shift_y == 2 * side_y - 1
    by_y = jnp.where(out_x, shift_y, 0)
    by_x = jnp.where(out_y, shift_x, 0)

    def table(head, tail):
        return head, tail

    def east_rows():
        cell = lax.broadcasted_iota(I32, (1, WIDE), 1)
        index = jnp.where(side_x == 0, ei[0:1, :], ei[1:2, :])
        upper = (index - (gy * LANES + third(cell)) + 1).astype(F32)
        weight = jnp.where(side_x == 0, ew[0:1, :], ew[1:2, :])
        wide = (LEVELS, WIDE)
        return jnp.broadcast_to(upper, wide), jnp.broadcast_to(weight, wide)

    def east_parents(b, f):
        return eb[pl.ds(side_x * 48 + f * 16 + b, LEVELS, stride=2), :]

    def north_parents(b, f):
        return nbw[pl.ds(side_y * 48 + f * 16 + b, LEVELS, stride=2), :]

    @pl.when(x_edge)
    def _():
        acc = jnp.zeros((LEVELS, LANES), F32)
        for b in range(2):
            for f in range(3):
                k = 3 * b + f
                near = (((lane - 8 * k + 4) & 127) >> 3) == 0
                acc = jnp.where(near, roll(east_parents(b, f), 8 * k), acc)
        east_out[0] = acc
        upper, weight = east_rows()
        first = lax.broadcasted_iota(I32, (LEVELS, LANES), 0) == 0
        rows = []
        for v in (upper, weight):
            rows.append(jnp.where(lane < 96, roll(v[:, 0:LANES], 64), v[:, 2 * LANES : WIDE]))
        east_out[1] = jnp.where(first, rows[0], rows[1])

    @pl.when(y_edge)
    def _():
        nbw[...] = jnp.zeros((96, LANES), F32)
        nbw[:, 0:8] = nb[...]
        cell = lax.broadcasted_iota(I32, (2, ROWS), 1)
        ntab[...] = jnp.zeros((LEVELS, LANES), F32)
        ntab[0:2, 0:ROWS] = (ni[...] - (gx * 8 + third(cell)) + 1).astype(F32)
        ntab[2:4, 0:ROWS] = nw[...]
        acc = jnp.zeros((LEVELS, LANES), F32)
        for b in range(2):
            for f in range(3):
                k = 3 * b + f
                acc = jnp.where((lane >> 3) == k, roll(north_parents(b, f), 8 * k), acc)
        north_out[0] = acc
        north_out[1] = ntab[...]

    def to(dx, dy, src, dst, send, recv):
        return pltpu.make_async_remote_copy(
            src_ref=src,
            dst_ref=dst,
            send_sem=send,
            recv_sem=recv,
            device_id=(gx + dx, gy + dy),
            device_id_type=MESH,
        )

    sends = []
    for s, dy in enumerate((-1, 1)):
        sends.append((0, dy, has(0, dy), [to(0, dy, packed, from_y.at[1 - s], y_send.at[s], y_recv.at[1 - s])]))
    for a, dx in enumerate((-1, 1)):
        for s, dy in enumerate((-1, 1)):
            sends.append(
                (
                    dx,
                    dy,
                    has(dx, dy),
                    [to(dx, dy, packed.at[a], from_d.at[1 - a, 1 - s], d_send.at[2 * a + s], d_recv.at[2 * (1 - a) + 1 - s])],
                )
            )
    east_sends = []
    for s, dy in enumerate((-1, 1)):
        east_sends.append(
            (dy, jnp.logical_and(x_edge, has(0, dy)), to(0, dy, east_out, east_in.at[1 - s], ea_send.at[s], ea_recv.at[1 - s]))
        )
    x_sends = []
    north_sends = []
    for a, dx in enumerate((-1, 1)):
        group = []
        for f in range(3):
            n = X_ROWS[f]
            if dx < 0:
                src, dst = ext.at[f, HALO : HALO + n], ext.at[f, HALO + ROWS : HALO + ROWS + n]
            else:
                src, dst = ext.at[f, HALO + ROWS - n : HALO + ROWS], ext.at[f, HALO - n : HALO]
            group.append(to(dx, 0, src, dst, x_send.at[3 * a + f], x_recv.at[3 * (1 - a) + f]))
        x_sends.append((dx, 0, has(dx, 0), group))
        north_sends.append(
            (dx, jnp.logical_and(y_edge, has(dx, 0)), to(dx, 0, north_out, north_in.at[1 - a], na_send.at[a], na_recv.at[1 - a]))
        )

    count_x = 1 + has_x[-1].astype(I32) + has_x[1].astype(I32)
    count_y = 1 + has_y[-1].astype(I32) + has_y[1].astype(I32)
    pl.semaphore_wait(barrier, count_x * count_y - 1)

    for _, _, there, group in sends:

        @pl.when(there)
        def _(group=group):
            for c in group:
                c.start()

    for _, there, c in east_sends + north_sends:

        @pl.when(there)
        def _(c=c):
            c.start()

    for _, _, there, group in x_sends:

        @pl.when(there)
        def _(group=group):
            for c in group:
                c.start()

    level = lax.broadcasted_iota(I32, (LEVELS, LANES), 0)
    half = jnp.zeros((LEVELS, LANES), F32)
    visc = jnp.zeros((LEVELS, LANES), F32)
    for l in range(LEVELS):
        half = jnp.where(level == l, 0.5 * ks[l], half)
        visc = jnp.where(level == l, qs[l], visc)
    half_w = jnp.concatenate([half] * 3, axis=1)
    visc_w = jnp.concatenate([visc] * 3, axis=1)

    def in_first(r):
        x = gx * ROWS + r - HALO
        return jnp.where(jnp.logical_and(x >= 3 * shift_x, x < total_x + 3 * shift_x), 1.0, 0.0).astype(F32)

    def in_second(r):
        x = gx * ROWS + r - HALO
        return jnp.where(jnp.logical_and(x >= 0, x < total_x), 1.0, 0.0).astype(F32)

    def store_mid(f, r, v):
        mid[f, r] = v

    def store_out(f, r, v):
        out[f, r - HALO] = v

    def substep_1(lo, hi):
        advance(lambda f, r: ext[f, r], store_mid, lo, hi, half_w, lambda r: half_w * in_first(r), visc_w, 1)

    def substep_2(lo, hi):
        advance(lambda f, r: mid[f, r], store_out, lo, hi, half_w, lambda r: half_w * in_second(r), visc_w, 1)

    substep_1(9, 23)
    substep_2(11, 21)

    def blend(parents, base, upper, weight, by):
        c0 = (1.0 - upper) * (1.0 - weight)
        c1 = (1.0 - upper) * weight + upper * (1.0 - weight)
        c2 = upper * weight
        values = []
        for v in parents:
            v = pick_shift(v, by, 1)
            values.append(c0 * take(v, base - 1) + c1 * take(v, base) + c2 * take(v, base + 1))
        return values

    def outward(c):
        return jnp.where(side_x > 0, (2.0 * c + 1.0) / 6.0, (5.0 - 2.0 * c) / 6.0).astype(F32)

    @pl.when(x_edge)
    def _():
        upper, weight = east_rows()
        upper = pick_shift(upper, by_y, 3)
        weight = pick_shift(weight, by_y, 3)
        for j in range(3):
            cut = slice(LANES * j, LANES * j + LANES)
            base = third(lane + LANES * j)
            for f in range(3):
                inner, outer = blend([east_parents(b, f) for b in range(2)], base, upper[:, cut], weight[:, cut], by_y)
                for c in range(3):
                    a = outward(c)
                    strip[c, f, :, cut] = inner * (1.0 - a) + outer * a

    for a, (dx, _, there, group) in enumerate(x_sends):

        @pl.when(has(-dx, 0))
        def _(group=group):
            for c in group:
                c.wait_recv()

    for side, first_strip, first_own, zero in ((0, 1, 4, 0), (1, 28, 25, 31)):

        @pl.when(west if side == 0 else east)
        def _(first_strip=first_strip, first_own=first_own, zero=zero):
            for f in range(3):
                ext[f, zero] = jnp.zeros((LEVELS, WIDE), F32)
                for c in range(3):
                    ext[f, first_strip + c] = jnp.where(out_x, strip[c, f], 0.0)
                    ext[f, first_own + c] = jnp.where(out_x, ext[f, first_own + c], 0.0)

    for r in list(range(HALO)) + list(range(HALO + ROWS, SPAN)):
        for f in range(3):
            gxt[f, r] = edge_block(ext[f, r, :, 0:LANES], ext[f, r, :, 2 * LANES : WIDE])

    substep_1(2, 9)
    substep_1(23, 30)

    def lay_rows(dst, source, width):
        for side, first_own, beyond in ((0, 4, (2, 3)), (1, 25, (28, 29))):

            @pl.when(west if side == 0 else east)
            def _(first_own=first_own, beyond=beyond):
                for f in range(3):
                    for r in beyond:
                        dst[f, r] = jnp.zeros((LEVELS, width), F32)
                    for c in range(3):
                        dst[f, first_own + c] = jnp.where(out_x, dst[f, first_own + c], source[c, f])

    lay_rows(mid, strip, WIDE)
    substep_2(4, 11)
    substep_2(21, 28)

    @pl.when(y_edge)
    def _():
        for a, (dx, there, c) in enumerate(north_sends):

            @pl.when(has(-dx, 0))
            def _(c=c):
                c.wait_recv()

        lower_in = jnp.where(has_x[-1], north_in[0], 0.0)
        upper_in = jnp.where(has_x[1], north_in[1], 0.0)
        lower_tab = jnp.where(has_x[-1], north_in[0, 1], 0.0)
        upper_tab = jnp.where(has_x[1], north_in[1, 1], 0.0)
        lower_band, upper_band = lower_in[0], upper_in[0]
        own = ntab[...]
        tab = jnp.where(
            lane >= 112,
            roll(lower_tab, 128 - ROWS),
            jnp.where((lane >= ROWS) & (lane < 2 * ROWS), roll(upper_tab, ROWS), own),
        )
        tab = pick_shift(tab, by_x, 3)
        parents = []
        for b in range(2):
            for f in range(3):
                k = 3 * b + f
                v = jnp.where((lane >= 8) & (lane < 16), roll(upper_band, 8 - 8 * k), north_parents(b, f))
                parents.append(jnp.where(lane >= 120, roll(lower_band, -8 - 8 * k), v))
        place = lane & 7
        step = jnp.where(place < 4, place, place - 5).astype(F32)
        a = jnp.where(place < 4, (2.0 * step + 1.0) / 6.0, (5.0 - 2.0 * step) / 6.0)
        real = (place != 3) & (place != 4)
        for h in range(2):
            x = slot + (16 * h - HALO)
            base = third(x)
            tab_x = take(tab, x)
            upper = jnp.broadcast_to(jnp.where(side_y == 0, tab_x[0:1], tab_x[1:2]), (LEVELS, LANES))
            weight = jnp.broadcast_to(jnp.where(side_y == 0, tab_x[2:3], tab_x[3:4]), (LEVELS, LANES))
            whole = x + gx * ROWS - 3 * by_x
            fits = real & (whole >= 0) & (whole < total_x)
            values = blend(parents, base, upper, weight, by_x)
            for f in range(3):
                ns[h, f] = jnp.where(fits, values[f] * (1.0 - a) + values[3 + f] * a, 0.0)

    for s, (_, dy, _, group) in enumerate(sends):

        @pl.when(has(-sends[s][0], -dy) if sends[s][0] else has(0, -dy))
        def _(group=group):
            for c in group:
                c.wait_recv()

    low = (lane & 7) < 4
    halo_lanes = ((lane >= 64) & (lane < 68)) | (lane >= 124)
    cells = edge_cells() + gy * WIDE
    keep_north = jnp.logical_and(low, north)
    keep_south = jnp.logical_and(jnp.logical_not(low), south)
    ns_lanes = jnp.logical_or(keep_north, keep_south)
    joined = {}
    for f in range(3):
        for h in range(2):
            v = jnp.where(low, from_y[1, h, f], from_y[0, h, f])
            d = roll(jnp.where(low, from_d[h, 1, f], from_d[h, 0, f]), 64)
            v = jnp.where((slot < HALO) if h == 0 else (slot >= 16 - HALO), d, v)
            joined[h, f] = v
    for f in range(3):
        for h in range(2):
            packed_ns = jnp.where(out_y, ns[h, f], 0.0)
            joined[h, f] = jnp.where(ns_lanes, packed_ns, joined[h, f])
    for r in range(SPAN):
        h, i = divmod(r, 16)
        for f in range(3):
            gxt[f, r] = jnp.where(halo_lanes, roll(joined[h, f], -8 * i), gxt[f, r])

    @pl.when(x_edge)
    def _():
        for s, (dy, _, c) in enumerate(east_sends):

            @pl.when(has(0, -dy))
            def _(c=c):
                c.wait_recv()

        lower_in = jnp.where(has_y[-1], east_in[0], 0.0)
        upper_in = jnp.where(has_y[1], east_in[1], 0.0)
        lower_band, lower_tab = lower_in[0], lower_in[1]
        upper_band, upper_tab = upper_in[0], upper_in[1]
        upper, weight = east_rows()
        tabs = []
        for k, v in enumerate((upper, weight)):
            v = edge_block(v[:, 0:LANES], v[:, 2 * LANES : WIDE])
            lo_row = jnp.broadcast_to(lower_tab[k : k + 1], (LEVELS, LANES))
            up_row = jnp.broadcast_to(upper_tab[k : k + 1], (LEVELS, LANES))
            v = jnp.where((lane >= 64) & (lane < 96), up_row, v)
            v = jnp.where(lane >= 112, lo_row, v)
            tabs.append(pick_shift(v, by_y, 3))
        base = jnp.where(lane < 32, third(lane), jnp.where(lane < 96, third(lane + (WIDE - 64)) - 32, third(lane - LANES)))
        inside = jnp.logical_and(
            jnp.logical_or(jnp.logical_not(north), lane < 64) | (lane >= 96),
            jnp.logical_or(jnp.logical_not(south), lane < 96),
        )
        for f in range(3):
            parents = []
            for b in range(2):
                k = 3 * b + f
                own = east_parents(b, f)
                v = jnp.where((lane >= 64) & (lane < 96), roll(own, -32), own)
                v = jnp.where((lane >= 96) & (lane < 100), roll(upper_band, 96 - 8 * k), v)
                parents.append(jnp.where(lane >= 124, roll(lower_band, -8 * k), v))
            inner, outer = blend(parents, base, tabs[0], tabs[1], by_y)
            for c in range(3):
                a = outward(c)
                strip_g[c, f] = inner * (1.0 - a) + outer * a
        for side, first_strip, first_own, zero in ((0, 1, 4, 0), (1, 28, 25, 31)):

            @pl.when(west if side == 0 else east)
            def _(first_strip=first_strip, first_own=first_own, zero=zero):
                for f in range(3):
                    gxt[f, zero] = jnp.zeros((LEVELS, LANES), F32)
                    for c in range(3):
                        gxt[f, first_strip + c] = jnp.where(
                            inside, jnp.where(out_x, strip_g[c, f], 0.0), gxt[f, first_strip + c]
                        )
                        gxt[f, first_own + c] = jnp.where(out_x, gxt[f, first_own + c], 0.0)

    my_first = jnp.logical_and(cells >= 3 * shift_y, cells < total_y + 3 * shift_y)
    my_second = jnp.logical_and(cells >= 0, cells < total_y)

    @pl.when(y_edge)
    def _():
        for r in range(SPAN):
            for f in range(3):
                gxt[f, r] = jnp.where(my_first, gxt[f, r], 0.0)

    half_1 = jnp.where(my_first, half, 0.0)
    half_2 = jnp.where(my_second, half, 0.0)

    def store_midg(f, r, v):
        midg[f, r] = v

    def store_edge(f, r, v):
        r = r - HALO
        head = slice(0, LANES)
        tail = slice(2 * LANES, WIDE)
        out[f, r, :, head] = jnp.where(lane < 16, v, out[f, r, :, head])
        out[f, r, :, tail] = jnp.where(lane >= 112, roll(v, 64), out[f, r, :, tail])

    advance(lambda f, r: gxt[f, r], store_midg, 2, 30, half, lambda r: half_1 * in_first(r), visc, None)
    lay_rows(midg, strip_g, LANES)

    @pl.when(y_edge)
    def _():
        mine = jnp.where(north, jnp.where((lane >= 61) & (lane < 64), 1, 0), jnp.where(lane < 3, 1, 0)) > 0
        lay = jnp.logical_and(mine, jnp.logical_not(out_y))
        for r in range(2, 30):
            h, i = divmod(r, 16)
            for f in range(3):
                v = ns[h, f]
                v = jnp.where(north, roll(v, -8 * i - 3), roll(v, -8 * i + 3))
                v = jnp.where(lay, v, midg[f, r])
                midg[f, r] = jnp.where(my_second, v, 0.0)

    advance(lambda f, r: midg[f, r], store_edge, 4, 28, half, lambda r: half_2 * in_second(r), visc, None)

    for _, _, there, group in sends + x_sends:

        @pl.when(there)
        def _(group=group):
            for c in group:
                c.wait_send()

    for _, there, c in east_sends + north_sends:

        @pl.when(there)
        def _(c=c):
            c.wait_send()


def write_kernel(ready, out, sem):
    copies = [
        pltpu.make_async_copy(ready.at[f, :, l, :], out.at[f, l], sem.at[f * LEVELS + l])
        for f in range(3)
        for l in range(LEVELS)
    ]
    for c in copies:
        c.start()
    for c in copies:
        c.wait()


def body(
    sizes,
    fields,
    east_band,
    north_band,
    east_index,
    north_index,
    east_weight,
    north_weight,
    nest_moves,
    courant,
    diffuse,
):
    vmem = pltpu.VMEM
    dma = pltpu.SemaphoreType.DMA
    tile = (LEVELS, LANES)
    ready = pl.pallas_call(
        functools.partial(exchange_kernel, sizes),
        out_shape=jax.ShapeDtypeStruct((3, ROWS, LEVELS, WIDE), F32),
        in_specs=[pl.BlockSpec(memory_space=pl.ANY)] * 10,
        out_specs=pl.BlockSpec(memory_space=pltpu.VMEM),
        scratch_shapes=[
            vmem((3, SPAN, LEVELS, WIDE), F32),
            vmem((3, SPAN) + tile, F32),
            vmem((3, SPAN, LEVELS, WIDE), F32),
            vmem((3, SPAN) + tile, F32),
            vmem((2, 3) + tile, F32),
            vmem((2, 2, 3) + tile, F32),
            vmem((2, 2, 3) + tile, F32),
            vmem((2,) + tile, F32),
            vmem((2, 2) + tile, F32),
            vmem((2,) + tile, F32),
            vmem((2, 2) + tile, F32),
            vmem((3, 3, LEVELS, WIDE), F32),
            vmem((3, 3) + tile, F32),
            vmem((2, 3) + tile, F32),
            vmem((96, LANES), F32),
            vmem((2, WIDE), I32),
            vmem((2, WIDE), F32),
            vmem((96, 8), F32),
            vmem((96, LANES), F32),
            vmem((2, ROWS), I32),
            vmem((2, ROWS), F32),
            vmem(tile, F32),
            pltpu.SMEM((2, 2), I32),
            pltpu.SMEM((LEVELS,), F32),
            pltpu.SMEM((LEVELS,), F32),
            dma((24,)),
            dma((9,)),
            dma((6,)),
            dma((6,)),
            dma((2,)),
            dma((2,)),
            dma((4,)),
            dma((4,)),
            dma((2,)),
            dma((2,)),
            dma((2,)),
            dma((2,)),
        ],
        compiler_params=pltpu.CompilerParams(
            collective_id=0, has_side_effects=True, vmem_limit_bytes=VMEM_A
        ),
    )(
        fields,
        east_band.reshape(96, LANES),
        north_band.reshape(96, 8),
        east_index,
        north_index,
        east_weight,
        north_weight,
        nest_moves,
        courant,
        diffuse,
    )
    return pl.pallas_call(
        write_kernel,
        out_shape=jax.ShapeDtypeStruct(fields.shape, F32),
        in_specs=[pl.BlockSpec(memory_space=pltpu.VMEM)],
        out_specs=pl.BlockSpec(memory_space=pl.ANY),
        scratch_shapes=[dma((24,))],
        compiler_params=pltpu.CompilerParams(vmem_limit_bytes=VMEM_B),
    )(ready)


VMEM_A = 56 * 1024 * 1024
VMEM_B = 8 * 1024 * 1024


def solution(mesh):
    sizes = (mesh.shape["gx"], mesh.shape["gy"])
    return jax.shard_map(
        functools.partial(body, sizes),
        mesh=mesh,
        in_specs=(
            P(None, None, "gx", "gy"),
            P(None, None, None, None, "gy"),
            P(None, None, None, None, "gx"),
            P(None, "gy"),
            P(None, "gx"),
            P(None, "gy"),
            P(None, "gx"),
            P(),
            P(),
            P(),
        ),
        out_specs=P(None, None, "gx", "gy"),
        check_vma=False,
    )
```

time: 244 us -> 21.4 us (0.09)
  the two profiles are of different devices: /device:TPU:95 before, /device:TPU:31 now
where the time goes in v1:
time: 21.4 us; the launch traced here: 21.2 us
  Pallas kernels  20 us (93%)
  local copies, waits for them, and re-layouts  1.16 us (5%)
    pallas_call x1, Pallas kernels, body(): pl.pallas_call(functools.partial(exchange_kernel, sizes), out_shape=jax.S...  18.9 us
    unnamed x2, local copies, waits for them, and re-layouts  1.16 us
    pallas_call x1, Pallas kernels, body(): pl.pallas_call(write_kernel, out_shape=jax.ShapeDtypeStruct(fields.shape,...  1.11 us

profile of v1, /device:TPU:31, one launch (start us, length us, event | category | flops | bytes accessed | tf_op | source)
XLA Modules:
  0.0 21.2 jit_solution(15241381392234992940)
XLA Ops:
  0.0 18.9 %shard_map.100.ready = f32[3,24,8,384]{3,2,1,0:T(8,128)} custom-call(f32[3,8,24,384]{3,2,1,0:T(8,128)} %fields.1, f32[96,128]{1,0:T(8,128)} %bitcast.2, f32[96,8]{1,0:T(8,128)} %bitcast.3, s32[2,384]{1,0:T(2,128)} %east_index.1, s32[2,24]{1,0:T(2,128)} %north_index.1, f32[2,384]{1,0:T(2,128)} %east_weight.1, f32[2,24]{1,0:T(2,128)} %north_weight.1, ...), custom_call_target="tpu_custom_call" | custom-call | tf_op jit(solution)/shard_map/pallas_call | solution.py:630
  18.9 0.0 copy-start
  18.9 1.2 %copy-done = f32[3,24,8,384]{3,2,1,0:T(8,128)S(1)} copy-done((f32[3,24,8,384]{3,2,1,0:T(8,128)S(1)}, f32[3,24,8,384]{3,2,1,0:T(8,128)}, u32[]{:S(2)}) %copy-start) | copy-done | bytes 884760
  20.1 1.1 %shard_map.101 = f32[3,8,24,384]{3,2,1,0:T(8,128)} custom-call(f32[3,24,8,384]{3,2,1,0:T(8,128)S(1)} %copy-done), custom_call_target="tpu_custom_call" | custom-call | tf_op jit(solution)/shard_map/pallas_call | solution.py:689
Async XLA Ops:
  18.9 1.2 %copy-start = (f32[3,24,8,384]{3,2,1,0:T(8,128)S(1)}, f32[3,24,8,384]{3,2,1,0:T(8,128)}, u32[]{:S(2)}) copy-start(f32[3,24,8,384]{3,2,1,0:T(8,128)} %shard_map.100.ready) | copy-start | bytes 2654212

commit v2 on v1

v2 whole, which is shorter than its diff:
```python
import functools

import jax
import jax.numpy as jnp
from jax import lax
from jax.experimental import pallas as pl
from jax.experimental.pallas import tpu as pltpu
from jax.sharding import PartitionSpec as P

MESH = pl.DeviceIdType.MESH
F32 = jnp.float32
I32 = jnp.int32
HALO = 4
ROWS = 24
SPAN = ROWS + 2 * HALO
WIDE = 384
LANES = 128
LEVELS = 8
X_ROWS = (4, 3, 2)
TILE = (LEVELS, LANES)


def third(v):
    return (((v + 48) * 43691) >> 17) - 16


def roll(v, by):
    by = by % v.shape[1]
    return pltpu.roll(v, by, 1) if by else v


def roll_rows(v, by):
    return pltpu.roll(v, by % v.shape[0], 0)


def iota(axis=1, shape=TILE):
    return lax.broadcasted_iota(I32, shape, axis)


def take(v, at):
    return jnp.take_along_axis(v, at & (LANES - 1), axis=1)


def pick_shift(v, by, step):
    return jnp.where(by > 0, roll(v, step), jnp.where(by < 0, roll(v, -step), v))


def slots():
    lane = iota()
    return jnp.where((lane & 7) < 4, ((lane + 64) & 127) >> 3, ((lane + 4) & 127) >> 3)


def advance(load, store, lo, hi, kk, kk_row, visc):
    def first(r, p_below, p_here, p_above):
        k = kk_row(r)
        u = load(1, r) - k * (p_above - p_below)
        v = load(2, r) - k * (roll(p_here, -1) - roll(p_here, 1))
        return u, v

    p = [load(0, lo - 2 + i) for i in range(4)]
    ub, vb = first(lo - 1, p[0], p[1], p[2])
    u0, v0 = first(lo, p[1], p[2], p[3])
    p0, p1 = p[2], p[3]
    for r in range(lo, hi):
        p2 = load(0, r + 2)
        ua, va = first(r + 1, p0, p1, p2)
        un, us, vn, vs = roll(u0, -1), roll(u0, 1), roll(v0, -1), roll(v0, 1)
        store(0, r, p0 - kk * ((ua - ub) + (vn - vs)))
        store(1, r, u0 + visc * (((ua + ub) + (un + us)) - 4.0 * u0))
        store(2, r, v0 + visc * (((va + vb) + (vn + vs)) - 4.0 * v0))
        p0, p1, ub, u0, vb, v0 = p1, p2, u0, ua, v0, va


def edge_substep(fields, kk_in, kk, visc):
    p, u, v = fields
    u = u - kk_in * (roll_rows(p, -1) - roll_rows(p, 1))
    v = v - kk_in * (roll(p, -1) - roll(p, 1))
    ue, uw = roll_rows(u, -1), roll_rows(u, 1)
    vn, vs = roll(v, -1), roll(v, 1)
    p = p - kk * ((ue - uw) + (vn - vs))
    u2 = u + visc * (((ue + uw) + (roll(u, -1) + roll(u, 1))) - 4.0 * u)
    v2 = v + visc * (((roll_rows(v, -1) + roll_rows(v, 1)) + (vn + vs)) - 4.0 * v)
    return p, u2, v2


def exchange_kernel(
    sizes,
    fields,
    east_band,
    north_band,
    east_index,
    north_index,
    east_weight,
    north_weight,
    moves,
    courant,
    diffuse,
    nat,
    ext,
    mid,
    gl,
    gr,
    to_y,
    from_y,
    from_d,
    east_out,
    east_in,
    north_out,
    north_in,
    strip,
    stage,
    sg,
    ns,
    ns_stage,
    nsa,
    eb,
    ei,
    ew,
    nb,
    nbw,
    ni,
    nw,
    ntab,
    mv,
    ks,
    qs,
    in_sem,
    small_sem,
    x_send,
    x_recv,
    y_send,
    y_recv,
    d_send,
    d_recv,
    ea_send,
    ea_recv,
    na_send,
    na_recv,
    ready,
):
    nx, ny = sizes
    gx = lax.axis_index("gx")
    gy = lax.axis_index("gy")
    total_x = nx * ROWS
    total_y = ny * WIDE
    upper_mid = ny // 2
    lower_mid = upper_mid - 1
    west, east = gx == 0, gx == nx - 1
    south, north = gy == 0, gy == ny - 1
    x_edge = jnp.logical_or(west, east)
    y_edge = jnp.logical_or(south, north)
    has_x = {-1: gx > 0, 1: gx < nx - 1}
    has_y = {-1: gy > 0, 1: gy < ny - 1}
    at_lower = gy == lower_mid
    at_upper = gy == upper_mid
    at_mid = jnp.logical_or(at_lower, at_upper)

    def both(a, b):
        return jnp.logical_and(a, b)

    def has(dx, dy):
        if dx and dy:
            return both(has_x[dx], has_y[dy])
        return has_x[dx] if dx else has_y[dy]

    def over(dy):
        return at_lower if dy > 0 else at_upper

    around = [(dx, dy) for dy in (-1, 1, 0) for dx in (-1, 0, 1) if dx or dy]
    barrier = pltpu.get_barrier_semaphore()
    for dx, dy in around:
        if dy:
            to_mid = (gy + dy == lower_mid) if dy > 0 else (gy + dy == upper_mid)
            greet = both(has(dx, dy), jnp.logical_or(over(dy), jnp.logical_not(to_mid)))
        else:
            greet = both(has(dx, dy), jnp.logical_not(at_mid))

        @pl.when(greet)
        def _(dx=dx, dy=dy):
            pl.semaphore_signal(barrier, inc=1, device_id=(gx + dx, gy + dy), device_id_type=MESH)

    loads = [
        pltpu.make_async_copy(
            fields.at[f, l, :, LANES * j : LANES * j + LANES], ext.at[j, f, 0:ROWS, l, :], in_sem.at[3 * j + f]
        )
        for j in (0, 2, 1)
        for f in range(3)
        for l in range(LEVELS)
    ]
    smalls = [
        pltpu.make_async_copy(s, d, small_sem.at[k])
        for k, (s, d) in enumerate(
            (
                (moves, mv),
                (courant, ks),
                (diffuse, qs),
                (east_band, eb),
                (east_index, ei),
                (east_weight, ew),
                (north_band, nb),
                (north_index, ni),
                (north_weight, nw),
            )
        )
    ]
    for c in loads + smalls:
        c.start()

    def wait_load(j, f):
        block = ext.at[j, f, 0:ROWS]
        pltpu.make_async_copy(block, block, in_sem.at[3 * j + f]).wait()

    for j in (0, 2):
        for f in range(3):
            wait_load(j, f)

    lane = iota()
    part = lane & 15
    ext_rows = ext.reshape(9 * SPAN * LEVELS, LANES)

    def edge_windows(t):
        for f in range(3):
            low, high = None, None
            for l in range(LEVELS):
                at = (f * SPAN + 8 * t) * LEVELS + l
                head = ext_rows[pl.ds(at, 8, stride=LEVELS), :]
                tail = ext_rows[pl.ds(at + 6 * SPAN * LEVELS, 8, stride=LEVELS), :]
                v = roll(jnp.where(lane < 64, head, tail), 16 * l + 4)
                low = v if low is None else jnp.where((lane >> 4) == l, v, low)
                high = v if high is None else jnp.where((((lane + 8) >> 4) & 7) == l, v, high)
            gl[f, 8 * t : 8 * t + 8] = low
            gr[f, 8 * t : 8 * t + 8] = high

    for t in range(3):
        edge_windows(t)
        for d, (source, shift) in enumerate(((gl, -4), (gr, 0))):
            v = roll(source[0, 8 * t : 8 * t + 8], shift)
            for f in range(1, 3):
                v = jnp.where((part >> 2) == f, roll(source[f, 8 * t : 8 * t + 8], 4 * f + shift), v)
            to_y[d, t] = v
    for c in smalls:
        c.wait()

    shift_x = mv[0, 0]
    shift_y = mv[0, 1]
    side_x = jnp.where(west, 0, 1)
    side_y = jnp.where(south, 0, 1)
    out_x = shift_x == 2 * side_x - 1
    out_y = shift_y == 2 * side_y - 1
    by_y = jnp.where(out_x, shift_y, 0)
    by_x = jnp.where(out_y, shift_x, 0)

    def east_rows():
        cell = iota(1, (1, WIDE))
        index = jnp.where(side_x == 0, ei[0:1, :], ei[1:2, :])
        upper = (index - (gy * LANES + third(cell)) + 1).astype(F32)
        weight = jnp.where(side_x == 0, ew[0:1, :], ew[1:2, :])
        wide = (LEVELS, WIDE)
        return jnp.broadcast_to(upper, wide), jnp.broadcast_to(weight, wide)

    def east_parents(b, f):
        return eb[pl.ds(side_x * 48 + f * 16 + b, LEVELS, stride=2), :]

    def north_parents(b, f):
        return nbw[pl.ds(side_y * 48 + f * 16 + b, LEVELS, stride=2), :]

    @pl.when(x_edge)
    def _():
        acc = jnp.zeros(TILE, F32)
        for b in range(2):
            for f in range(3):
                k = 3 * b + f
                near = (((lane - 8 * k + 4) & 127) >> 3) == 0
                acc = jnp.where(near, roll(east_parents(b, f), 8 * k), acc)
        east_out[0] = acc
        rows = [jnp.where(lane < 64, v[:, 0:LANES], v[:, 2 * LANES : WIDE]) for v in east_rows()]
        east_out[1] = jnp.where(iota(0) == 0, rows[0], rows[1])

    @pl.when(y_edge)
    def _():
        nbw[...] = jnp.zeros((96, LANES), F32)
        nbw[:, 0:8] = nb[...]
        cell = iota(1, (2, ROWS))
        ntab[...] = jnp.zeros(TILE, F32)
        ntab[0:2, 0:ROWS] = (ni[...] - (gx * 8 + third(cell)) + 1).astype(F32)
        ntab[2:4, 0:ROWS] = nw[...]
        acc = jnp.zeros(TILE, F32)
        for b in range(2):
            for f in range(3):
                k = 3 * b + f
                acc = jnp.where((lane >> 3) == k, roll(north_parents(b, f), 8 * k), acc)
        north_out[0] = acc
        north_out[1] = ntab[...]

    def to(dx, dy, src, dst, send, recv):
        return pltpu.make_async_remote_copy(
            src_ref=src,
            dst_ref=dst,
            send_sem=send,
            recv_sem=recv,
            device_id=(gx + dx, gy + dy),
            device_id_type=MESH,
        )

    y_sends = {}
    for s, dy in enumerate((-1, 1)):
        group = [(has(0, dy), to(0, dy, to_y.at[s], from_y.at[1 - s], y_send.at[s], y_recv.at[1 - s]), has(0, -dy))]
        for a, dx in enumerate((-1, 1)):
            c = to(dx, dy, to_y.at[s, 2 * a], from_d.at[1 - a, 1 - s], d_send.at[2 * a + s], d_recv.at[2 * (1 - a) + 1 - s])
            group.append((has(dx, dy), c, has(-dx, -dy)))
        c = to(0, dy, east_out, east_in.at[1 - s], ea_send.at[s], ea_recv.at[1 - s])
        group.append((both(x_edge, has(0, dy)), c, both(x_edge, has(0, -dy))))
        y_sends[dy] = group
    x_sends = []
    north_sends = []
    for a, dx in enumerate((-1, 1)):
        for f in range(3):
            n = X_ROWS[f]
            if dx < 0:
                src, dst = ext.at[:, f, 0:n], ext.at[:, f, ROWS : ROWS + n]
            else:
                src, dst = ext.at[:, f, ROWS - n : ROWS], ext.at[:, f, SPAN - n : SPAN]
            c = to(dx, 0, src, dst, x_send.at[3 * a + f], x_recv.at[3 * (1 - a) + f])
            x_sends.append((has(dx, 0), c, has(-dx, 0)))
        c = to(dx, 0, north_out, north_in.at[1 - a], na_send.at[a], na_recv.at[1 - a])
        north_sends.append((both(y_edge, has(dx, 0)), c, both(y_edge, has(-dx, 0))))

    def start(group, extra=None):
        for there, c, _ in group:

            @pl.when(there if extra is None else both(there, extra))
            def _(c=c):
                c.start()

    def wait_recv(group):
        for _, c, there in group:

            @pl.when(there)
            def _(c=c):
                c.wait_recv()

    count_x = 1 + has_x[-1].astype(I32) + has_x[1].astype(I32)
    count_y = 1 + has_y[-1].astype(I32) + has_y[1].astype(I32)

    for f in range(3):
        wait_load(1, f)

    @pl.when(at_upper)
    def _():
        pl.semaphore_wait(barrier, count_x)
        start(y_sends[-1])

    @pl.when(jnp.logical_not(at_mid))
    def _():
        pl.semaphore_wait(barrier, count_x * count_y - 1)

        @pl.when(gy == lower_mid - 1)
        def _():
            pl.semaphore_signal(ready, inc=1, device_id=(gx, gy + 1), device_id_type=MESH)

        @pl.when(gy == upper_mid + 1)
        def _():
            pl.semaphore_signal(ready, inc=1, device_id=(gx, gy - 1), device_id_type=MESH)

        start(y_sends[-1])
        start(y_sends[1])
        start(north_sends)
        start(x_sends)

    def spread(values, level, scale):
        v = jnp.zeros(TILE, F32)
        for l in range(LEVELS):
            v = jnp.where(level == l, scale * values[l], v)
        return v

    level = iota(0)
    half = spread(ks, level, 0.5)
    visc = spread(qs, level, 1.0)
    half_w = jnp.concatenate([half] * 3, axis=1)
    visc_w = jnp.concatenate([visc] * 3, axis=1)
    nat_rows = nat.reshape(9 * ROWS * LEVELS, LANES)

    def in_first(r):
        x = gx * ROWS + r
        return jnp.where(both(x >= 3 * shift_x, x < total_x + 3 * shift_x), 1.0, 0.0).astype(F32)

    def in_second(r):
        x = gx * ROWS + r
        return jnp.where(both(x >= 0, x < total_x), 1.0, 0.0).astype(F32)

    def load_ext(f, r):
        return jnp.concatenate([ext[j, f, r % SPAN] for j in range(3)], axis=1)

    def load_mid(f, r):
        return mid[f, r % SPAN]

    def store_mid(f, r, v):
        mid[f, r % SPAN] = v

    def store_nat(f, r, v):
        for j in range(3):
            at = (3 * j + f) * LEVELS * ROWS + r
            nat_rows[pl.ds(at, LEVELS, stride=ROWS), :] = v[:, LANES * j : LANES * j + LANES]

    def substep_1(lo, hi, kk_row):
        advance(load_ext, store_mid, lo, hi, half_w, kk_row, visc_w)

    def substep_2(lo, hi, kk_row):
        advance(load_mid, store_nat, lo, hi, half_w, kk_row, visc_w)

    def everywhere(r):
        return half_w

    substep_1(5, 19, everywhere)
    substep_2(7, 17, everywhere)

    @pl.when(at_mid)
    def _():
        pl.semaphore_wait(ready, 1)
        start(x_sends)
        start(y_sends[-1], at_lower)
        start(y_sends[1], at_upper)
        start(north_sends)

    @pl.when(at_lower)
    def _():
        pl.semaphore_wait(barrier, count_x)
        start(y_sends[1])

    def blend(parents, base, upper, weight, by):
        c0 = (1.0 - upper) * (1.0 - weight)
        c1 = (1.0 - upper) * weight + upper * (1.0 - weight)
        c2 = upper * weight
        values = []
        for v in parents:
            v = pick_shift(v, by, 1)
            values.append(c0 * take(v, base - 1) + c1 * take(v, base) + c2 * take(v, base + 1))
        return values

    def outward(c):
        return jnp.where(side_x > 0, (2.0 * c + 1.0) / 6.0, (5.0 - 2.0 * c) / 6.0).astype(F32)

    @pl.when(x_edge)
    def _():
        upper, weight = east_rows()
        upper = pick_shift(upper, by_y, 3)
        weight = pick_shift(weight, by_y, 3)
        for j in range(3):
            cut = slice(LANES * j, LANES * j + LANES)
            base = third(lane + LANES * j)
            for f in range(3):
                inner, outer = blend([east_parents(b, f) for b in range(2)], base, upper[:, cut], weight[:, cut], by_y)
                for c in range(3):
                    a = outward(c)
                    strip[c, f, :, cut] = inner * (1.0 - a) + outer * a

    tall = (SPAN, LANES)
    row = iota(0, tall)
    row = jnp.where(row < SPAN - HALO, row, row - SPAN) + gx * ROWS
    part_t = iota(1, tall) & 15
    in_x1 = (row >= 3 * shift_x) & (row < total_x + 3 * shift_x)
    in_x2 = (row >= 0) & (row < total_x)
    sides = []
    for window, origin in (((lane >> 4), -HALO), (((lane + 8) >> 4) & 7, WIDE - 12)):
        k = spread(ks, window, 0.5)
        q = spread(qs, window, 1.0)
        k = jnp.concatenate([k] * 4, axis=0)
        q = jnp.concatenate([q] * 4, axis=0)
        y = (part_t if origin < 0 else ((part_t + 8) & 15)) + (origin + gy * WIDE)
        in_y = (y >= 0) & (y < total_y)
        first = in_x1 & (y >= 3 * shift_y) & (y < total_y + 3 * shift_y)
        second = in_x2 & in_y
        sides.append((k, q, first, second, jnp.where(first, k, 0.0), jnp.where(second, k, 0.0), in_y))

    wait_recv(x_sends)

    sides_x = ((west, 29, 0, 28, (30, 31)), (east, 24, 21, 27, (24, 25)))
    for there, beyond, own, zero, _ in sides_x:

        @pl.when(there)
        def _(beyond=beyond, own=own, zero=zero):
            for f in range(3):
                for j in range(3):
                    cut = slice(LANES * j, LANES * j + LANES)
                    ext[j, f, zero] = jnp.zeros(TILE, F32)
                    for c in range(3):
                        ext[j, f, beyond + c] = jnp.where(out_x, strip[c, f, :, cut], 0.0)
                        ext[j, f, own + c] = jnp.where(out_x, ext[j, f, own + c], 0.0)

    edge_windows(3)

    def first_rows(r):
        return half_w * in_first(r)

    def second_rows(r):
        return half_w * in_second(r)

    substep_1(-2, 5, first_rows)
    substep_1(19, 26, first_rows)
    for there, _, own, _, outside in sides_x:

        @pl.when(there)
        def _(own=own, outside=outside):
            for f in range(3):
                for r in outside:
                    mid[f, r] = jnp.zeros((LEVELS, WIDE), F32)
                for c in range(3):
                    mid[f, own + c] = jnp.where(out_x, mid[f, own + c], strip[c, f])

    substep_2(0, 7, second_rows)
    substep_2(17, 24, second_rows)

    @pl.when(y_edge)
    def _():
        wait_recv(north_sends)
        lower_band = jnp.where(has_x[-1], north_in[0, 0], 0.0)
        upper_band = jnp.where(has_x[1], north_in[1, 0], 0.0)
        lower_tab = jnp.where(has_x[-1], north_in[0, 1], 0.0)
        upper_tab = jnp.where(has_x[1], north_in[1, 1], 0.0)
        tab = jnp.where(
            lane >= 112,
            roll(lower_tab, 128 - ROWS),
            jnp.where((lane >= ROWS) & (lane < 2 * ROWS), roll(upper_tab, ROWS), ntab[...]),
        )
        tab = pick_shift(tab, by_x, 3)
        parents = []
        for b in range(2):
            for f in range(3):
                k = 3 * b + f
                v = jnp.where((lane >= 8) & (lane < 16), roll(upper_band, 8 - 8 * k), north_parents(b, f))
                parents.append(jnp.where(lane >= 120, roll(lower_band, -8 - 8 * k), v))
        place = lane & 7
        slot = slots()
        step = jnp.where(place < 4, place, place - 5).astype(F32)
        a = jnp.where(place < 4, (2.0 * step + 1.0) / 6.0, (5.0 - 2.0 * step) / 6.0)
        real = (place != 3) & (place != 4)
        for h in range(2):
            x = slot + (16 * h - HALO)
            base = third(x)
            tab_x = take(tab, x)
            upper = jnp.broadcast_to(jnp.where(side_y == 0, tab_x[0:1], tab_x[1:2]), TILE)
            weight = jnp.broadcast_to(jnp.where(side_y == 0, tab_x[2:3], tab_x[3:4]), TILE)
            whole = x + gx * ROWS - 3 * by_x
            fits = real & (whole >= 0) & (whole < total_x)
            values = blend(parents, base, upper, weight, by_x)
            for f in range(3):
                v = jnp.where(fits, values[f] * (1.0 - a) + values[3 + f] * a, 0.0)
                ns[h, f] = jnp.where(north, roll(v, -64), roll(v, -124))
        for r in range(SPAN):
            h, i = divmod(r, 16)
            for f in range(3):
                ns_stage[f, (r - HALO) % SPAN] = roll(ns[h, f], -8 * i)
        staged = ns_stage.reshape(3 * SPAN * LEVELS, LANES)
        for t in range(4):
            v = jnp.zeros(TILE, F32)
            for f in range(3):
                for l in range(LEVELS):
                    rows = staged[pl.ds((f * SPAN + 8 * t) * LEVELS + l, 8, stride=LEVELS), :]
                    v = jnp.where((lane >> 2) == 4 * l + f, roll(rows, 16 * l + 4 * f), v)
            nsa[t] = v

    wait_recv(y_sends[-1])
    wait_recv(y_sends[1])

    @pl.when(x_edge)
    def _():
        lower_band = jnp.where(has_y[-1], east_in[0, 0], 0.0)
        upper_band = jnp.where(has_y[1], east_in[1, 0], 0.0)
        lower_tab = jnp.where(has_y[-1], east_in[0, 1], 0.0)
        upper_tab = jnp.where(has_y[1], east_in[1, 1], 0.0)
        tabs = east_rows()
        for s in range(2):
            near = []
            for k in range(2):
                if s == 0:
                    v = jnp.where(lane >= 112, jnp.broadcast_to(lower_tab[k : k + 1], TILE), tabs[k][:, 0:LANES])
                else:
                    v = jnp.where(lane < 16, jnp.broadcast_to(upper_tab[k : k + 1], TILE), tabs[k][:, 2 * LANES : WIDE])
                near.append(pick_shift(v, by_y, 3))
            cell = jnp.where(lane < 64, lane, lane - LANES) + (WIDE if s else 0)
            base = third(cell)
            for f in range(3):
                parents = []
                for b in range(2):
                    k = 3 * b + f
                    own = east_parents(b, f)
                    if s == 0:
                        v = jnp.where(lane >= 124, roll(lower_band, -8 * k), own)
                    else:
                        v = jnp.where(lane < 4, roll(upper_band, -8 * k), own)
                    parents.append(v)
                inner, outer = blend(parents, base, near[0], near[1], by_y)
                for c in range(3):
                    a = outward(c)
                    v = inner * (1.0 - a) + outer * a
                    stage[s, f, c] = v
                    stage[s, f, 5 + c] = v
                for c in (3, 4):
                    stage[s, f, c] = jnp.zeros(TILE, F32)
        staged = stage.reshape(2 * 3 * 8 * LEVELS, LANES)
        for s in range(2):
            for f in range(3):
                acc = None
                for l in range(LEVELS):
                    v = roll(staged[pl.ds((s * 3 + f) * 8 * LEVELS + l, 8, stride=LEVELS), :], 16 * l + 4)
                    window = (lane >> 4) if s == 0 else (((lane + 8) >> 4) & 7)
                    acc = v if acc is None else jnp.where(window == l, v, acc)
                sg[s, f] = acc

    sub = iota(0)
    outer_side = both(x_edge, True)
    beyond_rows = jnp.where(west, 1, 0) * (sub >= 4).astype(I32) + jnp.where(east, 1, 0) * (sub < 4).astype(I32) > 0
    own_low = both(both(west, jnp.logical_not(out_x)), outer_side)
    own_high = both(both(east, jnp.logical_not(out_x)), outer_side)
    results = []
    for s, source in enumerate((gl, gr)):
        k, q, first, second, k1, k2, in_y = sides[s]
        absent = south if s == 0 else north
        take_strip = both(absent, out_y)
        lay_strip = both(absent, jnp.logical_not(out_y))
        head = jnp.where(sub < 4, from_d[1, s], from_d[0, s])
        arrived = jnp.concatenate([from_y[s, 0], from_y[s, 1], from_y[s, 2], head], axis=0)
        packed = jnp.concatenate([nsa[t] for t in range(4)], axis=0)
        arrived = jnp.where(absent, packed, arrived)
        halo = (part_t < 4) if s == 0 else ((part_t >= 4) & (part_t < 8))
        state = []
        for f in range(3):
            v = jnp.where(halo, roll(arrived, -4 * f + 4 * s), source[f])
            tip = jnp.where(beyond_rows & in_y[0:8], sg[s, f], v[24:32])
            v = jnp.concatenate([v[0:24], tip], axis=0)
            state.append(jnp.where(first, v, 0.0))
        state = edge_substep(state, k1, k, q)
        if s == 0:
            own_strip = (part_t >= 4) & (part_t < 7)
        else:
            own_strip = (part_t >= 1) & (part_t < 4)
        own_strip = own_strip & lay_strip
        laid = []
        for f in range(3):
            v = state[f]
            low = jnp.where((sub < 3) & own_low, sg[s, f], v[0:8])
            high = jnp.where((sub >= 5) & own_high, sg[s, f], v[16:24])
            v = jnp.concatenate([low, v[8:16], high, v[24:32]], axis=0)
            v = jnp.where(own_strip, roll(packed, -4 * f + (3 if s == 0 else 1)), v)
            laid.append(jnp.where(second, v, 0.0))
        results.append(edge_substep(laid, k2, k, q))

    part_r = iota(1, (ROWS, LANES)) & 15
    lane_r = iota(1, (ROWS, LANES))
    for f in range(3):
        v = jnp.where((part_r >= 4) & (part_r < 12), results[0][f][0:ROWS], results[1][f][0:ROWS])
        for l in range(LEVELS):
            m = roll(v, -16 * l - 4)
            nat[0, f, l] = jnp.where(lane_r < 8, m, nat[0, f, l])
            nat[2, f, l] = jnp.where(lane_r >= 120, m, nat[2, f, l])

    for there, c, _ in y_sends[-1] + y_sends[1] + x_sends + north_sends:

        @pl.when(there)
        def _(c=c):
            c.wait_send()


def write_kernel(ready, out, sem):
    copies = [
        pltpu.make_async_copy(ready.at[j, f], out.at[f, :, :, LANES * j : LANES * j + LANES], sem.at[3 * j + f])
        for j in range(3)
        for f in range(3)
    ]
    for c in copies:
        c.start()
    for c in copies:
        c.wait()


def body(
    sizes,
    fields,
    east_band,
    north_band,
    east_index,
    north_index,
    east_weight,
    north_weight,
    nest_moves,
    courant,
    diffuse,
):
    vmem = pltpu.VMEM
    dma = pltpu.SemaphoreType.DMA
    ready = pl.pallas_call(
        functools.partial(exchange_kernel, sizes),
        out_shape=vmem((3, 3, LEVELS, ROWS, LANES), F32),
        in_specs=[pl.BlockSpec(memory_space=pl.ANY)] * 10,
        out_specs=pl.BlockSpec(memory_space=pltpu.VMEM),
        scratch_shapes=[
            vmem((3, 3, SPAN) + TILE, F32),
            vmem((3, SPAN, LEVELS, WIDE), F32),
            vmem((3, SPAN, LANES), F32),
            vmem((3, SPAN, LANES), F32),
            vmem((2, 3) + TILE, F32),
            vmem((2, 3) + TILE, F32),
            vmem((2, 2) + TILE, F32),
            vmem((2,) + TILE, F32),
            vmem((2, 2) + TILE, F32),
            vmem((2,) + TILE, F32),
            vmem((2, 2) + TILE, F32),
            vmem((3, 3, LEVELS, WIDE), F32),
            vmem((2, 3, 8) + TILE, F32),
            vmem((2, 3) + TILE, F32),
            vmem((2, 3) + TILE, F32),
            vmem((3, SPAN) + TILE, F32),
            vmem((4,) + TILE, F32),
            vmem((96, LANES), F32),
            vmem((2, WIDE), I32),
            vmem((2, WIDE), F32),
            vmem((96, 8), F32),
            vmem((96, LANES), F32),
            vmem((2, ROWS), I32),
            vmem((2, ROWS), F32),
            vmem(TILE, F32),
            pltpu.SMEM((2, 2), I32),
            pltpu.SMEM((LEVELS,), F32),
            pltpu.SMEM((LEVELS,), F32),
            dma((9,)),
            dma((9,)),
            dma((6,)),
            dma((6,)),
            dma((2,)),
            dma((2,)),
            dma((4,)),
            dma((4,)),
            dma((2,)),
            dma((2,)),
            dma((2,)),
            dma((2,)),
            pltpu.SemaphoreType.REGULAR,
        ],
        compiler_params=pltpu.CompilerParams(
            collective_id=0, has_side_effects=True, vmem_limit_bytes=VMEM_A
        ),
    )(
        fields,
        east_band.reshape(96, LANES),
        north_band.reshape(96, 8),
        east_index,
        north_index,
        east_weight,
        north_weight,
        nest_moves,
        courant,
        diffuse,
    )
    return pl.pallas_call(
        write_kernel,
        out_shape=jax.ShapeDtypeStruct(fields.shape, F32),
        in_specs=[pl.BlockSpec(memory_space=pltpu.VMEM)],
        out_specs=pl.BlockSpec(memory_space=pl.ANY),
        scratch_shapes=[dma((9,))],
        compiler_params=pltpu.CompilerParams(vmem_limit_bytes=VMEM_B),
    )(ready)


VMEM_A = 56 * 1024 * 1024
VMEM_B = 8 * 1024 * 1024


def solution(mesh):
    sizes = (mesh.shape["gx"], mesh.shape["gy"])
    return jax.shard_map(
        functools.partial(body, sizes),
        mesh=mesh,
        in_specs=(
            P(None, None, "gx", "gy"),
            P(None, None, None, None, "gy"),
            P(None, None, None, None, "gx"),
            P(None, "gy"),
            P(None, "gx"),
            P(None, "gy"),
            P(None, "gx"),
            P(),
            P(),
            P(),
        ),
        out_specs=P(None, None, "gx", "gy"),
        check_vma=False,
    )
```

time: 21.4 us -> 13.4 us (0.63)
  the two profiles are of different devices: /device:TPU:31 before, /device:TPU:193 now
where the time goes in v2:
time: 13.4 us; the launch traced here: 13.2 us
  Pallas kernels  13.2 us (99%)
    pallas_call x1, Pallas kernels, body(): pl.pallas_call(functools.partial(exchange_kernel, sizes), out_shape=vmem(...  12.2 us
    pallas_call x1, Pallas kernels, body(): pl.pallas_call(write_kernel, out_shape=jax.ShapeDtypeStruct(fields.shape,...  0.98 us

profile of v2, /device:TPU:193, one launch (start us, length us, event | category | flops | bytes accessed | tf_op | source)
XLA Modules:
  0.0 13.2 jit_solution(8743794758317800121)
XLA Ops:
  0.0 12.2 %shard_map.100.ready = f32[3,3,8,24,128]{4,3,2,1,0:T(8,128)S(1)} custom-call(f32[3,8,24,384]{3,2,1,0:T(8,128)} %fields.1, f32[96,128]{1,0:T(8,128)} %bitcast.2, f32[96,8]{1,0:T(8,128)} %bitcast.3, s32[2,384]{1,0:T(2,128)} %east_index.1, s32[2,24]{1,0:T(2,128)} %north_index.1, f32[2,384]{1,0:T(2,128)} %east_weight.1, f32[2,24]{1,0:T(2,128)} %north_weight.1, ...), custom_call_target="tpu_custom_call" | custom-call | tf_op jit(solution)/shard_map/pallas_call | solution.py:691
  12.3 1.0 %shard_map.101 = f32[3,8,24,384]{3,2,1,0:T(8,128)} custom-call(f32[3,3,8,24,128]{4,3,2,1,0:T(8,128)S(1)} %shard_map.100.ready), custom_call_target="tpu_custom_call" | custom-call | tf_op jit(solution)/shard_map/pallas_call | solution.py:754

commit v3 on v2

--- a/solution.py
+++ b/solution.py
@@ -50,7 +50,7 @@
     return jnp.where((lane & 7) < 4, ((lane + 64) & 127) >> 3, ((lane + 4) & 127) >> 3)
 
 
-def advance(load, store, lo, hi, kk, kk_row, visc):
+def advance(load, store, lo, count, kk, kk_row, visc):
     def first(r, p_below, p_here, p_above):
         k = kk_row(r)
         u = load(1, r) - k * (p_above - p_below)
@@ -61,7 +61,8 @@
     ub, vb = first(lo - 1, p[0], p[1], p[2])
     u0, v0 = first(lo, p[1], p[2], p[3])
     p0, p1 = p[2], p[3]
-    for r in range(lo, hi):
+    for step in range(count):
+        r = lo + step
         p2 = load(0, r + 2)
         ua, va = first(r + 1, p0, p1, p2)
         un, us, vn, vs = roll(u0, -1), roll(u0, 1), roll(v0, -1), roll(v0, 1)
@@ -71,15 +72,17 @@
         p0, p1, ub, u0, vb, v0 = p1, p2, u0, ua, v0, va
 
 
-def edge_substep(fields, kk_in, kk, visc):
+def edge_substep(fields, kk_in, kk, visc, keep):
     p, u, v = fields
     u = u - kk_in * (roll_rows(p, -1) - roll_rows(p, 1))
     v = v - kk_in * (roll(p, -1) - roll(p, 1))
-    ue, uw = roll_rows(u, -1), roll_rows(u, 1)
+    ue, uw = roll_rows(u, -1)[0:keep], roll_rows(u, 1)[0:keep]
+    ve, vw = roll_rows(v, -1)[0:keep], roll_rows(v, 1)[0:keep]
+    p, u, v, kk, visc = p[0:keep], u[0:keep], v[0:keep], kk[0:keep], visc[0:keep]
     vn, vs = roll(v, -1), roll(v, 1)
     p = p - kk * ((ue - uw) + (vn - vs))
     u2 = u + visc * (((ue + uw) + (roll(u, -1) + roll(u, 1))) - 4.0 * u)
-    v2 = v + visc * (((roll_rows(v, -1) + roll_rows(v, 1)) + (vn + vs)) - 4.0 * v)
+    v2 = v + visc * (((ve + vw) + (vn + vs)) - 4.0 * v)
     return p, u2, v2
 
 
@@ -98,8 +101,7 @@
     nat,
     ext,
     mid,
-    gl,
-    gr,
+    g,
     to_y,
     from_y,
     from_d,
@@ -112,7 +114,11 @@
     sg,
     ns,
     ns_stage,
-    nsa,
+    nso,
+    hop,
+    mask,
+    factor,
+    done,
     eb,
     ei,
     ew,
@@ -137,6 +143,8 @@
     na_send,
     na_recv,
     ready,
+    h_send,
+    h_recv,
 ):
     nx, ny = sizes
     gx = lax.axis_index("gx")
@@ -166,18 +174,27 @@
     def over(dy):
         return at_lower if dy > 0 else at_upper
 
-    around = [(dx, dy) for dy in (-1, 1, 0) for dx in (-1, 0, 1) if dx or dy]
+    odd = lax.rem(gx, 2) == 1
+    even = jnp.logical_not(odd)
+    is_far = {-1: even, 1: odd}
+    has_far = jnp.where(odd, has_x[1].astype(I32), has_x[-1].astype(I32))
+
     barrier = pltpu.get_barrier_semaphore()
-    for dx, dy in around:
-        if dy:
-            to_mid = (gy + dy == lower_mid) if dy > 0 else (gy + dy == upper_mid)
-            greet = both(has(dx, dy), jnp.logical_or(over(dy), jnp.logical_not(to_mid)))
-        else:
-            greet = both(has(dx, dy), jnp.logical_not(at_mid))
-
-        @pl.when(greet)
-        def _(dx=dx, dy=dy):
+
+    def greet(dx, dy, there):
+        @pl.when(both(has(dx, dy), there))
+        def _():
             pl.semaphore_signal(barrier, inc=1, device_id=(gx + dx, gy + dy), device_id_type=MESH)
+
+    for dy in (1, -1):
+        for dx in (-1, 1, 0):
+            greet(dx, dy, both(over(dy), is_far[dx]) if dx and dy < 0 else over(dy))
+    for dy in (1, -1):
+        to_mid = (gy + dy == lower_mid) if dy > 0 else (gy + dy == upper_mid)
+        for dx in (-1, 1, 0):
+            greet(dx, dy, jnp.logical_not(jnp.logical_or(over(dy), to_mid)))
+    for dx in (-1, 1):
+        greet(dx, 0, jnp.logical_not(at_mid))
 
     loads = [
         pltpu.make_async_copy(
@@ -228,15 +245,15 @@
                 v = roll(jnp.where(lane < 64, head, tail), 16 * l + 4)
                 low = v if low is None else jnp.where((lane >> 4) == l, v, low)
                 high = v if high is None else jnp.where((((lane + 8) >> 4) & 7) == l, v, high)
-            gl[f, 8 * t : 8 * t + 8] = low
-            gr[f, 8 * t : 8 * t + 8] = high
+            g[0, f, 8 * t : 8 * t + 8] = low
+            g[1, f, 8 * t : 8 * t + 8] = high
 
     for t in range(3):
         edge_windows(t)
-        for d, (source, shift) in enumerate(((gl, -4), (gr, 0))):
-            v = roll(source[0, 8 * t : 8 * t + 8], shift)
+        for d in range(2):
+            v = g[d, 0, 8 * t : 8 * t + 8]
             for f in range(1, 3):
-                v = jnp.where((part >> 2) == f, roll(source[f, 8 * t : 8 * t + 8], 4 * f + shift), v)
+                v = jnp.where((part >> 2) == f + 1 - d, roll(g[d, f, 8 * t : 8 * t + 8], 4 * f), v)
             to_y[d, t] = v
     for c in smalls:
         c.wait()
@@ -304,10 +321,15 @@
 
     y_sends = {}
     for s, dy in enumerate((-1, 1)):
-        group = [(has(0, dy), to(0, dy, to_y.at[s], from_y.at[1 - s], y_send.at[s], y_recv.at[1 - s]), has(0, -dy))]
+        group = []
         for a, dx in enumerate((-1, 1)):
             c = to(dx, dy, to_y.at[s, 2 * a], from_d.at[1 - a, 1 - s], d_send.at[2 * a + s], d_recv.at[2 * (1 - a) + 1 - s])
-            group.append((has(dx, dy), c, has(-dx, -dy)))
+            there = has(dx, dy)
+            if dy > 0:
+                there = both(there, jnp.logical_or(is_far[dx], jnp.logical_not(at_lower)))
+            group.append((there, c, has(-dx, -dy)))
+        c = to(0, dy, to_y.at[s], from_y.at[1 - s], y_send.at[s], y_recv.at[1 - s])
+        group.append((has(0, dy), c, has(0, -dy)))
         c = to(0, dy, east_out, east_in.at[1 - s], ea_send.at[s], ea_recv.at[1 - s])
         group.append((both(x_edge, has(0, dy)), c, both(x_edge, has(0, -dy))))
         y_sends[dy] = group
@@ -325,6 +347,13 @@
         c = to(dx, 0, north_out, north_in.at[1 - a], na_send.at[a], na_recv.at[1 - a])
         north_sends.append((both(y_edge, has(dx, 0)), c, both(y_edge, has(-dx, 0))))
 
+    side = jnp.where(at_upper, 1, 0)
+    east_one = odd.astype(I32)
+    mate = 1 - 2 * east_one
+    has_mate = jnp.where(odd, has_x[-1].astype(I32), has_x[1].astype(I32)) > 0
+    first_hop = to(mate, 0, to_y.at[1, 2 * (1 - east_one)], hop, h_send.at[0], h_recv)
+    last_hop = to(0, 1, hop, from_d.at[1 - east_one, 0], h_send.at[1], d_recv.at[2 * (1 - east_one)])
+
     def start(group, extra=None):
         for there, c, _ in group:
 
@@ -389,34 +418,39 @@
         return jnp.where(both(x >= 0, x < total_x), 1.0, 0.0).astype(F32)
 
     def load_ext(f, r):
-        return jnp.concatenate([ext[j, f, r % SPAN] for j in range(3)], axis=1)
+        return jnp.concatenate([ext[j, f, r & (SPAN - 1)] for j in range(3)], axis=1)
 
     def load_mid(f, r):
-        return mid[f, r % SPAN]
+        return mid[f, r & (SPAN - 1)]
 
     def store_mid(f, r, v):
-        mid[f, r % SPAN] = v
+        mid[f, r & (SPAN - 1)] = v
 
     def store_nat(f, r, v):
         for j in range(3):
             at = (3 * j + f) * LEVELS * ROWS + r
             nat_rows[pl.ds(at, LEVELS, stride=ROWS), :] = v[:, LANES * j : LANES * j + LANES]
 
-    def substep_1(lo, hi, kk_row):
-        advance(load_ext, store_mid, lo, hi, half_w, kk_row, visc_w)
-
-    def substep_2(lo, hi, kk_row):
-        advance(load_mid, store_nat, lo, hi, half_w, kk_row, visc_w)
+    def substep_1(lo, count, kk_row):
+        advance(load_ext, store_mid, lo, count, half_w, kk_row, visc_w)
+
+    def substep_2(lo, count, kk_row):
+        advance(load_mid, store_nat, lo, count, half_w, kk_row, visc_w)
 
     def everywhere(r):
         return half_w
 
-    substep_1(5, 19, everywhere)
-    substep_2(7, 17, everywhere)
+    substep_1(5, 14, everywhere)
+    substep_2(7, 10, everywhere)
 
     @pl.when(at_mid)
     def _():
         pl.semaphore_wait(ready, 1)
+
+        @pl.when(both(at_lower, has_mate))
+        def _():
+            first_hop.start()
+
         start(x_sends)
         start(y_sends[-1], at_lower)
         start(y_sends[1], at_upper)
@@ -424,8 +458,13 @@
 
     @pl.when(at_lower)
     def _():
-        pl.semaphore_wait(barrier, count_x)
+        pl.semaphore_wait(barrier, 1 + has_far)
         start(y_sends[1])
+
+        @pl.when(has_mate)
+        def _():
+            first_hop.wait_recv()
+            last_hop.start()
 
     def blend(parents, base, upper, weight, by):
         c0 = (1.0 - upper) * (1.0 - weight)
@@ -460,19 +499,14 @@
     part_t = iota(1, tall) & 15
     in_x1 = (row >= 3 * shift_x) & (row < total_x + 3 * shift_x)
     in_x2 = (row >= 0) & (row < total_x)
-    sides = []
-    for window, origin in (((lane >> 4), -HALO), (((lane + 8) >> 4) & 7, WIDE - 12)):
-        k = spread(ks, window, 0.5)
-        q = spread(qs, window, 1.0)
-        k = jnp.concatenate([k] * 4, axis=0)
-        q = jnp.concatenate([q] * 4, axis=0)
+    for s, (window, origin) in enumerate((((lane >> 4), -HALO), (((lane + 8) >> 4) & 7, WIDE - 12))):
+        factor[s, 0] = spread(ks, window, 0.5)
+        factor[s, 1] = spread(qs, window, 1.0)
         y = (part_t if origin < 0 else ((part_t + 8) & 15)) + (origin + gy * WIDE)
         in_y = (y >= 0) & (y < total_y)
-        first = in_x1 & (y >= 3 * shift_y) & (y < total_y + 3 * shift_y)
-        second = in_x2 & in_y
-        sides.append((k, q, first, second, jnp.where(first, k, 0.0), jnp.where(second, k, 0.0), in_y))
-
-    wait_recv(x_sends)
+        mask[s, 0] = jnp.where(in_x1 & (y >= 3 * shift_y) & (y < total_y + 3 * shift_y), 1.0, 0.0)
+        mask[s, 1] = jnp.where(in_x2 & in_y, 1.0, 0.0)
+        mask[s, 2] = jnp.where(in_y, 1.0, 0.0)
 
     sides_x = ((west, 29, 0, 28, (30, 31)), (east, 24, 21, 27, (24, 25)))
     for there, beyond, own, zero, _ in sides_x:
@@ -487,28 +521,37 @@
                         ext[j, f, beyond + c] = jnp.where(out_x, strip[c, f, :, cut], 0.0)
                         ext[j, f, own + c] = jnp.where(out_x, ext[j, f, own + c], 0.0)
 
-    edge_windows(3)
-
     def first_rows(r):
         return half_w * in_first(r)
 
     def second_rows(r):
         return half_w * in_second(r)
 
-    substep_1(-2, 5, first_rows)
-    substep_1(19, 26, first_rows)
-    for there, _, own, _, outside in sides_x:
-
-        @pl.when(there)
-        def _(own=own, outside=outside):
-            for f in range(3):
-                for r in outside:
-                    mid[f, r] = jnp.zeros((LEVELS, WIDE), F32)
-                for c in range(3):
-                    mid[f, own + c] = jnp.where(out_x, mid[f, own + c], strip[c, f])
-
-    substep_2(0, 7, second_rows)
-    substep_2(17, 24, second_rows)
+    for turn in range(2):
+        westward = odd if turn == 0 else even
+
+        @pl.when(westward)
+        def _():
+            wait_recv(x_sends[3:6])
+
+        @pl.when(jnp.logical_not(westward))
+        def _():
+            wait_recv(x_sends[0:3])
+
+        if turn == 1:
+            edge_windows(3)
+        substep_1(jnp.where(westward, -2, 19), 7, first_rows)
+        for there, _, own, _, outside in sides_x:
+
+            @pl.when(there)
+            def _(own=own, outside=outside):
+                for f in range(3):
+                    for r in outside:
+                        mid[f, r] = jnp.zeros((LEVELS, WIDE), F32)
+                    for c in range(3):
+                        mid[f, own + c] = jnp.where(out_x, mid[f, own + c], strip[c, f])
+
+        substep_2(jnp.where(westward, 0, 17), 7, second_rows)
 
     @pl.when(y_edge)
     def _():
@@ -545,114 +588,134 @@
             values = blend(parents, base, upper, weight, by_x)
             for f in range(3):
                 v = jnp.where(fits, values[f] * (1.0 - a) + values[3 + f] * a, 0.0)
-                ns[h, f] = jnp.where(north, roll(v, -64), roll(v, -124))
+                ns[h, f] = jnp.where(north, roll(v, -60), roll(v, -124))
         for r in range(SPAN):
             h, i = divmod(r, 16)
             for f in range(3):
                 ns_stage[f, (r - HALO) % SPAN] = roll(ns[h, f], -8 * i)
         staged = ns_stage.reshape(3 * SPAN * LEVELS, LANES)
+        late = jnp.where(north, 1, 0)
         for t in range(4):
             v = jnp.zeros(TILE, F32)
             for f in range(3):
                 for l in range(LEVELS):
                     rows = staged[pl.ds((f * SPAN + 8 * t) * LEVELS + l, 8, stride=LEVELS), :]
-                    v = jnp.where((lane >> 2) == 4 * l + f, roll(rows, 16 * l + 4 * f), v)
-            nsa[t] = v
-
-    wait_recv(y_sends[-1])
-    wait_recv(y_sends[1])
-
-    @pl.when(x_edge)
-    def _():
-        lower_band = jnp.where(has_y[-1], east_in[0, 0], 0.0)
-        upper_band = jnp.where(has_y[1], east_in[1, 0], 0.0)
-        lower_tab = jnp.where(has_y[-1], east_in[0, 1], 0.0)
-        upper_tab = jnp.where(has_y[1], east_in[1, 1], 0.0)
-        tabs = east_rows()
-        for s in range(2):
-            near = []
-            for k in range(2):
-                if s == 0:
-                    v = jnp.where(lane >= 112, jnp.broadcast_to(lower_tab[k : k + 1], TILE), tabs[k][:, 0:LANES])
-                else:
-                    v = jnp.where(lane < 16, jnp.broadcast_to(upper_tab[k : k + 1], TILE), tabs[k][:, 2 * LANES : WIDE])
-                near.append(pick_shift(v, by_y, 3))
-            cell = jnp.where(lane < 64, lane, lane - LANES) + (WIDE if s else 0)
-            base = third(cell)
+                    v = jnp.where((lane >> 2) == 4 * l + f + late, roll(rows, 16 * l + 4 * f), v)
+            for there, s in ((south, 0), (north, 1)):
+
+                @pl.when(there)
+                def _(s=s, t=t, v=v):
+                    if t < 3:
+                        from_y[s, t] = v
+                    else:
+                        from_d[0, s] = v
+                        from_d[1, s] = v
+
             for f in range(3):
-                parents = []
-                for b in range(2):
-                    k = 3 * b + f
-                    own = east_parents(b, f)
-                    if s == 0:
-                        v = jnp.where(lane >= 124, roll(lower_band, -8 * k), own)
-                    else:
-                        v = jnp.where(lane < 4, roll(upper_band, -8 * k), own)
-                    parents.append(v)
-                inner, outer = blend(parents, base, near[0], near[1], by_y)
-                for c in range(3):
-                    a = outward(c)
-                    v = inner * (1.0 - a) + outer * a
-                    stage[s, f, c] = v
-                    stage[s, f, 5 + c] = v
-                for c in (3, 4):
-                    stage[s, f, c] = jnp.zeros(TILE, F32)
-        staged = stage.reshape(2 * 3 * 8 * LEVELS, LANES)
-        for s in range(2):
-            for f in range(3):
-                acc = None
-                for l in range(LEVELS):
-                    v = roll(staged[pl.ds((s * 3 + f) * 8 * LEVELS + l, 8, stride=LEVELS), :], 16 * l + 4)
-                    window = (lane >> 4) if s == 0 else (((lane + 8) >> 4) & 7)
-                    acc = v if acc is None else jnp.where(window == l, v, acc)
-                sg[s, f] = acc
+                nso[f, 8 * t : 8 * t + 8] = jnp.where(north, roll(v, -4 * f - 3), roll(v, -4 * f + 3))
+
+    def east_edge_strip(s):
+        band = jnp.where(jnp.where(s == 0, has_y[-1], has_y[1]), east_in[s, 0], 0.0)
+        far_tab = jnp.where(jnp.where(s == 0, has_y[-1], has_y[1]), east_in[s, 1], 0.0)
+        beyond = ((lane + 64 * s) & 127) >= 64
+        near = []
+        for k, v in enumerate(east_rows()):
+            v = jnp.where(s == 0, v[:, 0:LANES], v[:, 2 * LANES : WIDE])
+            v = jnp.where(beyond, jnp.broadcast_to(far_tab[k : k + 1], TILE), v)
+            near.append(pick_shift(v, by_y, 3))
+        base = third(jnp.where(lane < 64, lane, lane - LANES) + WIDE * s)
+        for f in range(3):
+            parents = []
+            for b in range(2):
+                k = 3 * b + f
+                parents.append(jnp.where(beyond, roll(band, -8 * k), east_parents(b, f)))
+            inner, outer = blend(parents, base, near[0], near[1], by_y)
+            for c in range(3):
+                a = outward(c)
+                v = inner * (1.0 - a) + outer * a
+                stage[f, c] = v
+                stage[f, 5 + c] = v
+            for c in (3, 4):
+                stage[f, c] = jnp.zeros(TILE, F32)
+        staged = stage.reshape(3 * 8 * LEVELS, LANES)
+        window = ((lane + 8 * s) >> 4) & 7
+        for f in range(3):
+            acc = None
+            for l in range(LEVELS):
+                v = roll(staged[pl.ds(f * 8 * LEVELS + l, 8, stride=LEVELS), :], 16 * l + 4)
+                acc = v if acc is None else jnp.where(window == l, v, acc)
+            sg[f] = acc
 
     sub = iota(0)
-    outer_side = both(x_edge, True)
-    beyond_rows = jnp.where(west, 1, 0) * (sub >= 4).astype(I32) + jnp.where(east, 1, 0) * (sub < 4).astype(I32) > 0
-    own_low = both(both(west, jnp.logical_not(out_x)), outer_side)
-    own_high = both(both(east, jnp.logical_not(out_x)), outer_side)
-    results = []
-    for s, source in enumerate((gl, gr)):
-        k, q, first, second, k1, k2, in_y = sides[s]
-        absent = south if s == 0 else north
-        take_strip = both(absent, out_y)
-        lay_strip = both(absent, jnp.logical_not(out_y))
+    beyond_rows = (jnp.where(west, 1, 0) * (sub >= 4).astype(I32) + jnp.where(east, 1, 0) * (sub < 4).astype(I32)) > 0
+    own_low = both(west, jnp.logical_not(out_x))
+    own_high = both(east, jnp.logical_not(out_x))
+
+    def edge_side(s):
+        @pl.when(x_edge)
+        def _():
+            east_edge_strip(s)
+
+        k = jnp.concatenate([factor[s, 0]] * 4, axis=0)
+        q = jnp.concatenate([factor[s, 1]] * 4, axis=0)
+        first = mask[s, 0] > 0.5
+        second = mask[s, 1] > 0.5
+        in_y = mask[s, 2, 0:8] > 0.5
+        lay_strip = both(jnp.where(s == 0, south, north), jnp.logical_not(out_y))
         head = jnp.where(sub < 4, from_d[1, s], from_d[0, s])
         arrived = jnp.concatenate([from_y[s, 0], from_y[s, 1], from_y[s, 2], head], axis=0)
-        packed = jnp.concatenate([nsa[t] for t in range(4)], axis=0)
-        arrived = jnp.where(absent, packed, arrived)
-        halo = (part_t < 4) if s == 0 else ((part_t >= 4) & (part_t < 8))
+        halo = ((part_t - 4 * s) & 15) < 4
+        own_strip = (((part_t - 4 + 3 * s) & 15) < 3) & lay_strip
         state = []
         for f in range(3):
-            v = jnp.where(halo, roll(arrived, -4 * f + 4 * s), source[f])
-            tip = jnp.where(beyond_rows & in_y[0:8], sg[s, f], v[24:32])
+            v = jnp.where(halo, roll(arrived, -4 * f), g[s, f])
+            tip = jnp.where(beyond_rows & in_y, sg[f], v[24:32])
             v = jnp.concatenate([v[0:24], tip], axis=0)
             state.append(jnp.where(first, v, 0.0))
-        state = edge_substep(state, k1, k, q)
-        if s == 0:
-            own_strip = (part_t >= 4) & (part_t < 7)
-        else:
-            own_strip = (part_t >= 1) & (part_t < 4)
-        own_strip = own_strip & lay_strip
+        state = edge_substep(state, jnp.where(first, k, 0.0), k, q, SPAN)
         laid = []
         for f in range(3):
             v = state[f]
-            low = jnp.where((sub < 3) & own_low, sg[s, f], v[0:8])
-            high = jnp.where((sub >= 5) & own_high, sg[s, f], v[16:24])
+            low = jnp.where((sub < 3) & own_low, sg[f], v[0:8])
+            high = jnp.where((sub >= 5) & own_high, sg[f], v[16:24])
             v = jnp.concatenate([low, v[8:16], high, v[24:32]], axis=0)
-            v = jnp.where(own_strip, roll(packed, -4 * f + (3 if s == 0 else 1)), v)
+            v = jnp.where(own_strip, nso[f], v)
             laid.append(jnp.where(second, v, 0.0))
-        results.append(edge_substep(laid, k2, k, q))
-
-    part_r = iota(1, (ROWS, LANES)) & 15
+        return edge_substep(laid, jnp.where(second, k, 0.0), k, q, ROWS)
+
+    @pl.when(at_upper)
+    def _():
+        wait_recv(y_sends[-1])
+
+    @pl.when(jnp.logical_not(at_upper))
+    def _():
+        wait_recv(y_sends[1])
+
+    for f, v in enumerate(edge_side(side)):
+        done[f] = v
+
+    @pl.when(at_upper)
+    def _():
+        wait_recv(y_sends[1])
+
+    @pl.when(jnp.logical_not(at_upper))
+    def _():
+        wait_recv(y_sends[-1])
+
     lane_r = iota(1, (ROWS, LANES))
-    for f in range(3):
-        v = jnp.where((part_r >= 4) & (part_r < 12), results[0][f][0:ROWS], results[1][f][0:ROWS])
+    ahead = ((((lane_r & 15) + 12) & 15) < 8).astype(I32)
+    fresh = ahead == side
+    for f, v in enumerate(edge_side(1 - side)):
+        v = jnp.where(fresh, v, done[f])
         for l in range(LEVELS):
             m = roll(v, -16 * l - 4)
             nat[0, f, l] = jnp.where(lane_r < 8, m, nat[0, f, l])
             nat[2, f, l] = jnp.where(lane_r >= 120, m, nat[2, f, l])
+
+    @pl.when(both(at_lower, has_mate))
+    def _():
+        first_hop.wait_send()
+        last_hop.wait_send()
 
     for there, c, _ in y_sends[-1] + y_sends[1] + x_sends + north_sends:
 
@@ -696,8 +759,7 @@
         scratch_shapes=[
             vmem((3, 3, SPAN) + TILE, F32),
             vmem((3, SPAN, LEVELS, WIDE), F32),
-            vmem((3, SPAN, LANES), F32),
-            vmem((3, SPAN, LANES), F32),
+            vmem((2, 3, SPAN, LANES), F32),
             vmem((2, 3) + TILE, F32),
             vmem((2, 3) + TILE, F32),
             vmem((2, 2) + TILE, F32),
@@ -706,11 +768,15 @@
             vmem((2,) + TILE, F32),
             vmem((2, 2) + TILE, F32),
             vmem((3, 3, LEVELS, WIDE), F32),
-            vmem((2, 3, 8) + TILE, F32),
-            vmem((2, 3) + TILE, F32),
+            vmem((3, 8) + TILE, F32),
+            vmem((3,) + TILE, F32),
             vmem((2, 3) + TILE, F32),
             vmem((3, SPAN) + TILE, F32),
-            vmem((4,) + TILE, F32),
+            vmem((3, SPAN, LANES), F32),
+            vmem(TILE, F32),
+            vmem((2, 3, SPAN, LANES), F32),
+            vmem((2, 2) + TILE, F32),
+            vmem((3, ROWS, LANES), F32),
             vmem((96, LANES), F32),
             vmem((2, WIDE), I32),
             vmem((2, WIDE), F32),
@@ -735,6 +801,8 @@
             dma((2,)),
             dma((2,)),
             pltpu.SemaphoreType.REGULAR,
+            dma((2,)),
+            dma,
         ],
         compiler_params=pltpu.CompilerParams(
             collective_id=0, has_side_effects=True, vmem_limit_bytes=VMEM_A

time: 13.4 us -> 13.3 us (level)
  the two profiles are of different devices: /device:TPU:193 before, /device:TPU:192 now
where the time goes in v3:
time: 13.3 us; the launch traced here: 13.1 us
  Pallas kernels  13.1 us (98%)
    pallas_call x1, Pallas kernels, body(): pl.pallas_call(functools.partial(exchange_kernel, sizes), out_shape=vmem(...  12.1 us
    pallas_call x1, Pallas kernels, body(): pl.pallas_call(write_kernel, out_shape=jax.ShapeDtypeStruct(fields.shape,...  0.98 us

profile of v3, /device:TPU:192, one launch (start us, length us, event | category | flops | bytes accessed | tf_op | source)
XLA Modules:
  0.0 13.1 jit_solution(14719993921072042805)
XLA Ops:
  0.0 12.1 %shard_map.100.ready = f32[3,3,8,24,128]{4,3,2,1,0:T(8,128)S(1)} custom-call(f32[3,8,24,384]{3,2,1,0:T(8,128)} %fields.1, f32[96,128]{1,0:T(8,128)} %bitcast.2, f32[96,8]{1,0:T(8,128)} %bitcast.3, s32[2,384]{1,0:T(2,128)} %east_index.1, s32[2,24]{1,0:T(2,128)} %north_index.1, f32[2,384]{1,0:T(2,128)} %east_weight.1, f32[2,24]{1,0:T(2,128)} %north_weight.1, ...), custom_call_target="tpu_custom_call" | custom-call | tf_op jit(solution)/shard_map/pallas_call | solution.py:754
  12.1 1.0 %shard_map.101 = f32[3,8,24,384]{3,2,1,0:T(8,128)} custom-call(f32[3,3,8,24,128]{4,3,2,1,0:T(8,128)S(1)} %shard_map.100.ready), custom_call_target="tpu_custom_call" | custom-call | tf_op jit(solution)/shard_map/pallas_call | solution.py:822

commit v4 on v3

--- a/solution.py
+++ b/solution.py
@@ -17,6 +17,7 @@
 LANES = 128
 LEVELS = 8
 X_ROWS = (4, 3, 2)
+RUN = 8
 TILE = (LEVELS, LANES)
 
 
@@ -179,6 +180,9 @@
     is_far = {-1: even, 1: odd}
     has_far = jnp.where(odd, has_x[1].astype(I32), has_x[-1].astype(I32))
 
+    seam_west = both(lax.rem(gx, RUN) == 0, gx > 0)
+    seam_east = both(lax.rem(gx, RUN) == RUN - 1, gx < nx - 1)
+
     barrier = pltpu.get_barrier_semaphore()
 
     def greet(dx, dy, there):
@@ -188,7 +192,12 @@
 
     for dy in (1, -1):
         for dx in (-1, 1, 0):
-            greet(dx, dy, both(over(dy), is_far[dx]) if dx and dy < 0 else over(dy))
+            there = over(dy)
+            if dx and dy < 0:
+                there = both(there, is_far[dx])
+            if dx > 0 and dy < 0:
+                there = both(there, jnp.logical_not(seam_east))
+            greet(dx, dy, there)
     for dy in (1, -1):
         to_mid = (gy + dy == lower_mid) if dy > 0 else (gy + dy == upper_mid)
         for dx in (-1, 1, 0):
@@ -326,7 +335,9 @@
             c = to(dx, dy, to_y.at[s, 2 * a], from_d.at[1 - a, 1 - s], d_send.at[2 * a + s], d_recv.at[2 * (1 - a) + 1 - s])
             there = has(dx, dy)
             if dy > 0:
-                there = both(there, jnp.logical_or(is_far[dx], jnp.logical_not(at_lower)))
+                near = jnp.logical_not(is_far[dx])
+                near = jnp.logical_or(near, seam_west) if dx < 0 else near
+                there = both(there, jnp.logical_not(both(near, at_lower)))
             group.append((there, c, has(-dx, -dy)))
         c = to(0, dy, to_y.at[s], from_y.at[1 - s], y_send.at[s], y_recv.at[1 - s])
         group.append((has(0, dy), c, has(0, -dy)))
@@ -351,8 +362,10 @@
     east_one = odd.astype(I32)
     mate = 1 - 2 * east_one
     has_mate = jnp.where(odd, has_x[-1].astype(I32), has_x[1].astype(I32)) > 0
-    first_hop = to(mate, 0, to_y.at[1, 2 * (1 - east_one)], hop, h_send.at[0], h_recv)
-    last_hop = to(0, 1, hop, from_d.at[1 - east_one, 0], h_send.at[1], d_recv.at[2 * (1 - east_one)])
+    first_hop = to(mate, 0, to_y.at[1, 2 * (1 - east_one)], hop.at[0], h_send.at[0], h_recv.at[0])
+    last_hop = to(0, 1, hop.at[0], from_d.at[1 - east_one, 0], h_send.at[1], d_recv.at[2 * (1 - east_one)])
+    first_seam_hop = to(-1, 0, to_y.at[1, 0], hop.at[1], h_send.at[2], h_recv.at[1])
+    last_seam_hop = to(0, 1, hop.at[1], from_d.at[1, 0], h_send.at[3], d_recv.at[2])
 
     def start(group, extra=None):
         for there, c, _ in group:
@@ -451,6 +464,10 @@
         def _():
             first_hop.start()
 
+        @pl.when(both(at_lower, seam_west))
+        def _():
+            first_seam_hop.start()
+
         start(x_sends)
         start(y_sends[-1], at_lower)
         start(y_sends[1], at_upper)
@@ -458,13 +475,18 @@
 
     @pl.when(at_lower)
     def _():
-        pl.semaphore_wait(barrier, 1 + has_far)
+        pl.semaphore_wait(barrier, 1 + has_far - seam_west.astype(I32))
         start(y_sends[1])
 
         @pl.when(has_mate)
         def _():
             first_hop.wait_recv()
             last_hop.start()
+
+        @pl.when(seam_east)
+        def _():
+            first_seam_hop.wait_recv()
+            last_seam_hop.start()
 
     def blend(parents, base, upper, weight, by):
         c0 = (1.0 - upper) * (1.0 - weight)
@@ -694,6 +716,25 @@
     for f, v in enumerate(edge_side(side)):
         done[f] = v
 
+    for there, c, _ in y_sends[-1] + y_sends[1] + x_sends + north_sends:
+
+        @pl.when(there)
+        def _(c=c):
+            c.wait_send()
+
+    @pl.when(both(at_lower, has_mate))
+    def _():
+        first_hop.wait_send()
+        last_hop.wait_send()
+
+    @pl.when(both(at_lower, seam_west))
+    def _():
+        first_seam_hop.wait_send()
+
+    @pl.when(both(at_lower, seam_east))
+    def _():
+        last_seam_hop.wait_send()
+
     @pl.when(at_upper)
     def _():
         wait_recv(y_sends[1])
@@ -711,17 +752,6 @@
             m = roll(v, -16 * l - 4)
             nat[0, f, l] = jnp.where(lane_r < 8, m, nat[0, f, l])
             nat[2, f, l] = jnp.where(lane_r >= 120, m, nat[2, f, l])
-
-    @pl.when(both(at_lower, has_mate))
-    def _():
-        first_hop.wait_send()
-        last_hop.wait_send()
-
-    for there, c, _ in y_sends[-1] + y_sends[1] + x_sends + north_sends:
-
-        @pl.when(there)
-        def _(c=c):
-            c.wait_send()
 
 
 def write_kernel(ready, out, sem):
@@ -773,7 +803,7 @@
             vmem((2, 3) + TILE, F32),
             vmem((3, SPAN) + TILE, F32),
             vmem((3, SPAN, LANES), F32),
-            vmem(TILE, F32),
+            vmem((2,) + TILE, F32),
             vmem((2, 3, SPAN, LANES), F32),
             vmem((2, 2) + TILE, F32),
             vmem((3, ROWS, LANES), F32),
@@ -801,8 +831,8 @@
             dma((2,)),
             dma((2,)),
             pltpu.SemaphoreType.REGULAR,
+            dma((4,)),
             dma((2,)),
-            dma,
         ],
         compiler_params=pltpu.CompilerParams(
             collective_id=0, has_side_effects=True, vmem_limit_bytes=VMEM_A

time: 13.3 us -> 12.9 us (0.970)
  the two profiles are of different devices: /device:TPU:192 before, /device:TPU:27 now
where the time goes in v4:
time: 12.9 us; the launch traced here: 12.6 us
  Pallas kernels  12.6 us (98%)
    pallas_call x1, Pallas kernels, body(): pl.pallas_call(functools.partial(exchange_kernel, sizes), out_shape=vmem(...  11.6 us
    pallas_call x1, Pallas kernels, body(): pl.pallas_call(write_kernel, out_shape=jax.ShapeDtypeStruct(fields.shape,...  0.98 us

profile of v4, /device:TPU:27, one launch (start us, length us, event | category | flops | bytes accessed | tf_op | source)
XLA Modules:
  0.0 12.6 jit_solution(3804240067437241696)
XLA Ops:
  0.0 11.6 %shard_map.100.ready = f32[3,3,8,24,128]{4,3,2,1,0:T(8,128)S(1)} custom-call(f32[3,8,24,384]{3,2,1,0:T(8,128)} %fields.1, f32[96,128]{1,0:T(8,128)} %bitcast.2, f32[96,8]{1,0:T(8,128)} %bitcast.3, s32[2,384]{1,0:T(2,128)} %east_index.1, s32[2,24]{1,0:T(2,128)} %north_index.1, f32[2,384]{1,0:T(2,128)} %east_weight.1, f32[2,24]{1,0:T(2,128)} %north_weight.1, ...), custom_call_target="tpu_custom_call" | custom-call | tf_op jit(solution)/shard_map/pallas_call | solution.py:784
  11.7 1.0 %shard_map.101 = f32[3,8,24,384]{3,2,1,0:T(8,128)} custom-call(f32[3,3,8,24,128]{4,3,2,1,0:T(8,128)S(1)} %shard_map.100.ready), custom_call_target="tpu_custom_call" | custom-call | tf_op jit(solution)/shard_map/pallas_call | solution.py:852

commit v5 on v4

--- a/solution.py
+++ b/solution.py
@@ -131,21 +131,9 @@
     mv,
     ks,
     qs,
-    in_sem,
-    small_sem,
-    x_send,
-    x_recv,
-    y_send,
-    y_recv,
-    d_send,
-    d_recv,
-    ea_send,
-    ea_recv,
-    na_send,
-    na_recv,
+    sent,
+    received,
     ready,
-    h_send,
-    h_recv,
 ):
     nx, ny = sizes
     gx = lax.axis_index("gx")
@@ -207,38 +195,29 @@
 
     loads = [
         pltpu.make_async_copy(
-            fields.at[f, l, :, LANES * j : LANES * j + LANES], ext.at[j, f, 0:ROWS, l, :], in_sem.at[3 * j + f]
+            fields.at[f, l, :, LANES * j : LANES * j + LANES], ext.at[j, f, 0:ROWS, l, :], sent.at[j & 1]
         )
         for j in (0, 2, 1)
         for f in range(3)
         for l in range(LEVELS)
     ]
     smalls = [
-        pltpu.make_async_copy(s, d, small_sem.at[k])
+        pltpu.make_async_copy(s, d, sent.at[2 + k])
         for k, (s, d) in enumerate(
-            (
-                (moves, mv),
-                (courant, ks),
-                (diffuse, qs),
-                (east_band, eb),
-                (east_index, ei),
-                (east_weight, ew),
-                (north_band, nb),
-                (north_index, ni),
-                (north_weight, nw),
-            )
+            ((moves, mv), (courant, ks), (diffuse, qs), (east_band, eb), (east_index, ei), (east_weight, ew))
         )
+    ]
+    norths = [
+        pltpu.make_async_copy(s, d, sent.at[2 + k])
+        for k, (s, d) in enumerate(((north_band, nb), (north_index, ni), (north_weight, nw)))
     ]
     for c in loads + smalls:
         c.start()
 
-    def wait_load(j, f):
-        block = ext.at[j, f, 0:ROWS]
-        pltpu.make_async_copy(block, block, in_sem.at[3 * j + f]).wait()
-
-    for j in (0, 2):
-        for f in range(3):
-            wait_load(j, f)
+    def wait_bytes(block, sem):
+        pltpu.make_async_copy(block, block, sem).wait()
+
+    wait_bytes(ext.at[0:2, :, 0:ROWS], sent.at[0])
 
     lane = iota()
     part = lane & 15
@@ -304,6 +283,10 @@
 
     @pl.when(y_edge)
     def _():
+        for c in norths:
+            c.start()
+        for c in norths:
+            c.wait()
         nbw[...] = jnp.zeros((96, LANES), F32)
         nbw[:, 0:8] = nb[...]
         cell = iota(1, (2, ROWS))
@@ -332,16 +315,24 @@
     for s, dy in enumerate((-1, 1)):
         group = []
         for a, dx in enumerate((-1, 1)):
-            c = to(dx, dy, to_y.at[s, 2 * a], from_d.at[1 - a, 1 - s], d_send.at[2 * a + s], d_recv.at[2 * (1 - a) + 1 - s])
+            c = to(
+                dx,
+                dy,
+                to_y.at[s, 2 * a],
+                from_d.at[1 - a, 1 - s],
+                sent.at[4 + 2 * a + s],
+                received.at[4 + 2 * (1 - a) + 1 - s],
+            )
             there = has(dx, dy)
             if dy > 0:
                 near = jnp.logical_not(is_far[dx])
                 near = jnp.logical_or(near, seam_west) if dx < 0 else near
                 there = both(there, jnp.logical_not(both(near, at_lower)))
             group.append((there, c, has(-dx, -dy)))
-        c = to(0, dy, to_y.at[s], from_y.at[1 - s], y_send.at[s], y_recv.at[1 - s])
+        c = to(0, dy, to_y.at[s], from_y.at[1 - s], sent.at[2 + s], received.at[2 + 1 - s])
         group.append((has(0, dy), c, has(0, -dy)))
-        c = to(0, dy, east_out, east_in.at[1 - s], ea_send.at[s], ea_recv.at[1 - s])
+        send, recv = sent.at[4 + 2 * side_x + s], received.at[4 + 2 * side_x + 1 - s]
+        c = to(0, dy, east_out, east_in.at[1 - s], send, recv)
         group.append((both(x_edge, has(0, dy)), c, both(x_edge, has(0, -dy))))
         y_sends[dy] = group
     x_sends = []
@@ -353,19 +344,21 @@
                 src, dst = ext.at[:, f, 0:n], ext.at[:, f, ROWS : ROWS + n]
             else:
                 src, dst = ext.at[:, f, ROWS - n : ROWS], ext.at[:, f, SPAN - n : SPAN]
-            c = to(dx, 0, src, dst, x_send.at[3 * a + f], x_recv.at[3 * (1 - a) + f])
-            x_sends.append((has(dx, 0), c, has(-dx, 0)))
-        c = to(dx, 0, north_out, north_in.at[1 - a], na_send.at[a], na_recv.at[1 - a])
+            x_sends.append((has(dx, 0), to(dx, 0, src, dst, sent.at[a], received.at[1 - a]), None))
+        send, recv = sent.at[4 + 2 * a + side_y], received.at[4 + 2 * (1 - a) + side_y]
+        c = to(dx, 0, north_out, north_in.at[1 - a], send, recv)
         north_sends.append((both(y_edge, has(dx, 0)), c, both(y_edge, has(-dx, 0))))
 
     side = jnp.where(at_upper, 1, 0)
     east_one = odd.astype(I32)
     mate = 1 - 2 * east_one
     has_mate = jnp.where(odd, has_x[-1].astype(I32), has_x[1].astype(I32)) > 0
-    first_hop = to(mate, 0, to_y.at[1, 2 * (1 - east_one)], hop.at[0], h_send.at[0], h_recv.at[0])
-    last_hop = to(0, 1, hop.at[0], from_d.at[1 - east_one, 0], h_send.at[1], d_recv.at[2 * (1 - east_one)])
-    first_seam_hop = to(-1, 0, to_y.at[1, 0], hop.at[1], h_send.at[2], h_recv.at[1])
-    last_seam_hop = to(0, 1, hop.at[1], from_d.at[1, 0], h_send.at[3], d_recv.at[2])
+    first_hop = to(mate, 0, to_y.at[1, 2 * (1 - east_one)], hop.at[0], sent.at[8], received.at[8])
+    last_hop = to(
+        0, 1, hop.at[0], from_d.at[1 - east_one, 0], sent.at[4 + 2 * (1 - east_one) + 1], received.at[4 + 2 * (1 - east_one)]
+    )
+    first_seam_hop = to(-1, 0, to_y.at[1, 0], hop.at[1], sent.at[5], received.at[9])
+    last_seam_hop = to(0, 1, hop.at[1], from_d.at[1, 0], sent.at[9], received.at[6])
 
     def start(group, extra=None):
         for there, c, _ in group:
@@ -384,8 +377,7 @@
     count_x = 1 + has_x[-1].astype(I32) + has_x[1].astype(I32)
     count_y = 1 + has_y[-1].astype(I32) + has_y[1].astype(I32)
 
-    for f in range(3):
-        wait_load(1, f)
+    wait_bytes(ext.at[1, :, 0:ROWS], sent.at[1])
 
     @pl.when(at_upper)
     def _():
@@ -549,16 +541,21 @@
     def second_rows(r):
         return half_w * in_second(r)
 
+    def x_wait(sem, there):
+        @pl.when(there)
+        def _():
+            wait_bytes(ext.at[:, 0, 0 : sum(X_ROWS)], sem)
+
     for turn in range(2):
         westward = odd if turn == 0 else even
 
         @pl.when(westward)
         def _():
-            wait_recv(x_sends[3:6])
+            x_wait(received.at[0], has(-1, 0))
 
         @pl.when(jnp.logical_not(westward))
         def _():
-            wait_recv(x_sends[0:3])
+            x_wait(received.at[1], has(1, 0))
 
         if turn == 1:
             edge_windows(3)
@@ -716,7 +713,9 @@
     for f, v in enumerate(edge_side(side)):
         done[f] = v
 
-    for there, c, _ in y_sends[-1] + y_sends[1] + x_sends + north_sends:
+    for a, dx in enumerate((-1, 1)):
+        x_wait(sent.at[a], has(dx, 0))
+    for there, c, _ in y_sends[-1] + y_sends[1] + north_sends:
 
         @pl.when(there)
         def _(c=c):
@@ -755,15 +754,9 @@
 
 
 def write_kernel(ready, out, sem):
-    copies = [
-        pltpu.make_async_copy(ready.at[j, f], out.at[f, :, :, LANES * j : LANES * j + LANES], sem.at[3 * j + f])
-        for j in range(3)
-        for f in range(3)
-    ]
-    for c in copies:
-        c.start()
-    for c in copies:
-        c.wait()
+    for j in range(3):
+        pltpu.make_async_copy(ready.at[j], out.at[:, :, :, LANES * j : LANES * j + LANES], sem).start()
+    pltpu.make_async_copy(ready, ready, sem).wait()
 
 
 def body(
@@ -818,21 +811,9 @@
             pltpu.SMEM((2, 2), I32),
             pltpu.SMEM((LEVELS,), F32),
             pltpu.SMEM((LEVELS,), F32),
-            dma((9,)),
-            dma((9,)),
-            dma((6,)),
-            dma((6,)),
-            dma((2,)),
-            dma((2,)),
-            dma((4,)),
-            dma((4,)),
-            dma((2,)),
-            dma((2,)),
-            dma((2,)),
-            dma((2,)),
+            dma((10,)),
+            dma((10,)),
             pltpu.SemaphoreType.REGULAR,
-            dma((4,)),
-            dma((2,)),
         ],
         compiler_params=pltpu.CompilerParams(
             collective_id=0, has_side_effects=True, vmem_limit_bytes=VMEM_A
@@ -854,7 +835,7 @@
         out_shape=jax.ShapeDtypeStruct(fields.shape, F32),
         in_specs=[pl.BlockSpec(memory_space=pltpu.VMEM)],
         out_specs=pl.BlockSpec(memory_space=pl.ANY),
-        scratch_shapes=[dma((9,))],
+        scratch_shapes=[dma],
         compiler_params=pltpu.CompilerParams(vmem_limit_bytes=VMEM_B),
     )(ready)
 

time: 12.9 us -> 12.5 us (0.969)
  the two profiles are of different devices: /device:TPU:27 before, /device:TPU:224 now
where the time goes in v5:
time: 12.5 us; the launch traced here: 12.3 us
  Pallas kernels  12.3 us (98%)
    pallas_call x1, Pallas kernels, body(): pl.pallas_call(functools.partial(exchange_kernel, sizes), out_shape=vmem(...  11.4 us
    pallas_call x1, Pallas kernels, body(): pl.pallas_call(write_kernel, out_shape=jax.ShapeDtypeStruct(fields.shape,...  0.92 us

profile of v5, /device:TPU:224, one launch (start us, length us, event | category | flops | bytes accessed | tf_op | source)
XLA Modules:
  0.0 12.3 jit_solution(7389610975837860937)
XLA Ops:
  0.0 11.4 %shard_map.100.ready = f32[3,3,8,24,128]{4,3,2,1,0:T(8,128)S(1)} custom-call(f32[3,8,24,384]{3,2,1,0:T(8,128)} %fields.1, f32[96,128]{1,0:T(8,128)} %bitcast.2, f32[96,8]{1,0:T(8,128)} %bitcast.3, s32[2,384]{1,0:T(2,128)} %east_index.1, s32[2,24]{1,0:T(2,128)} %north_index.1, f32[2,384]{1,0:T(2,128)} %east_weight.1, f32[2,24]{1,0:T(2,128)} %north_weight.1, ...), custom_call_target="tpu_custom_call" | custom-call | tf_op jit(solution)/shard_map/pallas_call | solution.py:777
  11.4 0.9 %shard_map.101 = f32[3,8,24,384]{3,2,1,0:T(8,128)} custom-call(f32[3,3,8,24,128]{4,3,2,1,0:T(8,128)S(1)} %shard_map.100.ready), custom_call_target="tpu_custom_call" | custom-call | tf_op jit(solution)/shard_map/pallas_call | solution.py:833

commit v6 on v5

--- a/solution.py
+++ b/solution.py
@@ -73,18 +73,26 @@
         p0, p1, ub, u0, vb, v0 = p1, p2, u0, ua, v0, va
 
 
-def edge_substep(fields, kk_in, kk, visc, keep):
-    p, u, v = fields
-    u = u - kk_in * (roll_rows(p, -1) - roll_rows(p, 1))
-    v = v - kk_in * (roll(p, -1) - roll(p, 1))
-    ue, uw = roll_rows(u, -1)[0:keep], roll_rows(u, 1)[0:keep]
-    ve, vw = roll_rows(v, -1)[0:keep], roll_rows(v, 1)[0:keep]
-    p, u, v, kk, visc = p[0:keep], u[0:keep], v[0:keep], kk[0:keep], visc[0:keep]
-    vn, vs = roll(v, -1), roll(v, 1)
-    p = p - kk * ((ue - uw) + (vn - vs))
-    u2 = u + visc * (((ue + uw) + (roll(u, -1) + roll(u, 1))) - 4.0 * u)
-    v2 = v + visc * (((ve + vw) + (vn + vs)) - 4.0 * v)
-    return p, u2, v2
+def edge_substep(p, u, v, k_in, kk, visc, keep):
+    def across(w):
+        return roll_rows(w, -1), roll_rows(w, 1)
+
+    def first(i, rows):
+        east, west = across(p[i])
+        u1 = u[i][0:rows] - k_in[i][0:rows] * (east - west)[0:rows]
+        v1 = v[i][0:rows] - k_in[i][0:rows] * (p[i + 1][0:rows] - p[i - 1][0:rows])
+        return u1, v1
+
+    u0, v0 = first(0, SPAN)
+    un, vn = first(1, keep)
+    us, vs = first(-1, keep)
+    (ue, uw), (ve, vw) = ([w[0:keep] for w in across(x)] for x in (u0, v0))
+    u0, v0, kk, visc = u0[0:keep], v0[0:keep], kk[0:keep], visc[0:keep]
+    return (
+        p[0][0:keep] - kk * ((ue - uw) + (vn - vs)),
+        u0 + visc * (((ue + uw) + (un + us)) - 4.0 * u0),
+        v0 + visc * (((ve + vw) + (vn + vs)) - 4.0 * v0),
+    )
 
 
 def exchange_kernel(
@@ -117,6 +125,7 @@
     ns_stage,
     nso,
     hop,
+    pre,
     mask,
     factor,
     done,
@@ -151,6 +160,9 @@
     at_lower = gy == lower_mid
     at_upper = gy == upper_mid
     at_mid = jnp.logical_or(at_lower, at_upper)
+    under_lower = gy == lower_mid - 1
+    above_upper = gy == upper_mid + 1
+    at_next = jnp.logical_or(under_lower, above_upper)
 
     def both(a, b):
         return jnp.logical_and(a, b)
@@ -165,11 +177,12 @@
 
     odd = lax.rem(gx, 2) == 1
     even = jnp.logical_not(odd)
-    is_far = {-1: even, 1: odd}
-    has_far = jnp.where(odd, has_x[1].astype(I32), has_x[-1].astype(I32))
 
     seam_west = both(lax.rem(gx, RUN) == 0, gx > 0)
     seam_east = both(lax.rem(gx, RUN) == RUN - 1, gx < nx - 1)
+
+    last_column = lax.rem(gx, RUN) == RUN - 1
+    beside_last = lax.rem(gx, RUN) == RUN - 2
 
     barrier = pltpu.get_barrier_semaphore()
 
@@ -181,13 +194,12 @@
     for dy in (1, -1):
         for dx in (-1, 1, 0):
             there = over(dy)
-            if dx and dy < 0:
-                there = both(there, is_far[dx])
             if dx > 0 and dy < 0:
-                there = both(there, jnp.logical_not(seam_east))
+                there = both(there, jnp.logical_not(jnp.logical_or(seam_east, beside_last)))
             greet(dx, dy, there)
     for dy in (1, -1):
-        to_mid = (gy + dy == lower_mid) if dy > 0 else (gy + dy == upper_mid)
+        ahead = (gy + dy == lower_mid - 1) if dy > 0 else (gy + dy == upper_mid + 1)
+        to_mid = (under_lower if dy > 0 else above_upper) | ahead
         for dx in (-1, 1, 0):
             greet(dx, dy, jnp.logical_not(jnp.logical_or(over(dy), to_mid)))
     for dx in (-1, 1):
@@ -324,10 +336,8 @@
                 received.at[4 + 2 * (1 - a) + 1 - s],
             )
             there = has(dx, dy)
-            if dy > 0:
-                near = jnp.logical_not(is_far[dx])
-                near = jnp.logical_or(near, seam_west) if dx < 0 else near
-                there = both(there, jnp.logical_not(both(near, at_lower)))
+            if dx < 0 and dy > 0:
+                there = both(there, jnp.logical_not(both(at_lower, jnp.logical_or(seam_west, last_column))))
             group.append((there, c, has(-dx, -dy)))
         c = to(0, dy, to_y.at[s], from_y.at[1 - s], sent.at[2 + s], received.at[2 + 1 - s])
         group.append((has(0, dy), c, has(0, -dy)))
@@ -352,10 +362,9 @@
     side = jnp.where(at_upper, 1, 0)
     east_one = odd.astype(I32)
     mate = 1 - 2 * east_one
-    has_mate = jnp.where(odd, has_x[-1].astype(I32), has_x[1].astype(I32)) > 0
     first_hop = to(mate, 0, to_y.at[1, 2 * (1 - east_one)], hop.at[0], sent.at[8], received.at[8])
     last_hop = to(
-        0, 1, hop.at[0], from_d.at[1 - east_one, 0], sent.at[4 + 2 * (1 - east_one) + 1], received.at[4 + 2 * (1 - east_one)]
+        0, 1, hop.at[0], from_d.at[1 - east_one, 0], sent.at[8], received.at[4 + 2 * (1 - east_one)]
     )
     first_seam_hop = to(-1, 0, to_y.at[1, 0], hop.at[1], sent.at[5], received.at[9])
     last_seam_hop = to(0, 1, hop.at[1], from_d.at[1, 0], sent.at[9], received.at[6])
@@ -383,21 +392,24 @@
     def _():
         pl.semaphore_wait(barrier, count_x)
         start(y_sends[-1])
+        pl.semaphore_wait(ready, 1)
+        start(x_sends)
+        start(y_sends[1])
 
     @pl.when(jnp.logical_not(at_mid))
     def _():
-        pl.semaphore_wait(barrier, count_x * count_y - 1)
-
-        @pl.when(gy == lower_mid - 1)
+        pl.semaphore_wait(barrier, jnp.where(at_next, 2 * count_x, count_x * count_y) - 1)
+
+        @pl.when(jnp.logical_or(under_lower, gy == lower_mid - 2))
         def _():
             pl.semaphore_signal(ready, inc=1, device_id=(gx, gy + 1), device_id_type=MESH)
 
-        @pl.when(gy == upper_mid + 1)
+        @pl.when(jnp.logical_or(above_upper, gy == upper_mid + 2))
         def _():
             pl.semaphore_signal(ready, inc=1, device_id=(gx, gy - 1), device_id_type=MESH)
 
-        start(y_sends[-1])
-        start(y_sends[1])
+        start(y_sends[-1], jnp.logical_not(under_lower))
+        start(y_sends[1], jnp.logical_not(above_upper))
         start(north_sends)
         start(x_sends)
 
@@ -448,29 +460,33 @@
     substep_1(5, 14, everywhere)
     substep_2(7, 10, everywhere)
 
-    @pl.when(at_mid)
+    @pl.when(at_next)
     def _():
         pl.semaphore_wait(ready, 1)
-
-        @pl.when(both(at_lower, has_mate))
+        start(y_sends[-1], under_lower)
+        start(y_sends[1], above_upper)
+
+    @pl.when(at_lower)
+    def _():
+        pl.semaphore_wait(ready, 1)
+
+        @pl.when(last_column)
         def _():
             first_hop.start()
 
-        @pl.when(both(at_lower, seam_west))
+        @pl.when(seam_west)
         def _():
             first_seam_hop.start()
 
         start(x_sends)
-        start(y_sends[-1], at_lower)
-        start(y_sends[1], at_upper)
-        start(north_sends)
+        start(y_sends[-1])
 
     @pl.when(at_lower)
     def _():
-        pl.semaphore_wait(barrier, 1 + has_far - seam_west.astype(I32))
+        pl.semaphore_wait(barrier, count_x - jnp.logical_or(seam_west, last_column).astype(I32))
         start(y_sends[1])
 
-        @pl.when(has_mate)
+        @pl.when(beside_last)
         def _():
             first_hop.wait_recv()
             last_hop.start()
@@ -517,10 +533,12 @@
         factor[s, 0] = spread(ks, window, 0.5)
         factor[s, 1] = spread(qs, window, 1.0)
         y = (part_t if origin < 0 else ((part_t + 8) & 15)) + (origin + gy * WIDE)
-        in_y = (y >= 0) & (y < total_y)
-        mask[s, 0] = jnp.where(in_x1 & (y >= 3 * shift_y) & (y < total_y + 3 * shift_y), 1.0, 0.0)
-        mask[s, 1] = jnp.where(in_x2 & in_y, 1.0, 0.0)
-        mask[s, 2] = jnp.where(in_y, 1.0, 0.0)
+        for i in range(-2, 3):
+            z = y + i
+            in_y = (z >= 0) & (z < total_y)
+            mask[s, 0, i + 2] = jnp.where(in_x1 & (z >= 3 * shift_y) & (z < total_y + 3 * shift_y), 1.0, 0.0)
+            mask[s, 1, i + 2] = jnp.where(in_x2 & in_y, 1.0, 0.0)
+            mask[s, 2, i + 2] = jnp.where(in_y, 1.0, 0.0)
 
     sides_x = ((west, 29, 0, 28, (30, 31)), (east, 24, 21, 27, (24, 25)))
     for there, beyond, own, zero, _ in sides_x:
@@ -663,13 +681,21 @@
             for l in range(LEVELS):
                 v = roll(staged[pl.ds(f * 8 * LEVELS + l, 8, stride=LEVELS), :], 16 * l + 4)
                 acc = v if acc is None else jnp.where(window == l, v, acc)
-            sg[f] = acc
+            for i in range(-2, 3):
+                sg[f, i + 2] = roll(acc, -i)
 
     sub = iota(0)
     beyond_rows = (jnp.where(west, 1, 0) * (sub >= 4).astype(I32) + jnp.where(east, 1, 0) * (sub < 4).astype(I32)) > 0
     own_low = both(west, jnp.logical_not(out_x))
     own_high = both(east, jnp.logical_not(out_x))
 
+    reach = (2, 1, 1)
+
+    def edge_before(s):
+        for f in range(3):
+            for i in range(-reach[f], reach[f] + 1):
+                pre[f, i + 2] = roll(g[s, f], -i)
+
     def edge_side(s):
         @pl.when(x_edge)
         def _():
@@ -677,30 +703,35 @@
 
         k = jnp.concatenate([factor[s, 0]] * 4, axis=0)
         q = jnp.concatenate([factor[s, 1]] * 4, axis=0)
-        first = mask[s, 0] > 0.5
-        second = mask[s, 1] > 0.5
-        in_y = mask[s, 2, 0:8] > 0.5
         lay_strip = both(jnp.where(s == 0, south, north), jnp.logical_not(out_y))
         head = jnp.where(sub < 4, from_d[1, s], from_d[0, s])
         arrived = jnp.concatenate([from_y[s, 0], from_y[s, 1], from_y[s, 2], head], axis=0)
-        halo = ((part_t - 4 * s) & 15) < 4
         own_strip = (((part_t - 4 + 3 * s) & 15) < 3) & lay_strip
         state = []
         for f in range(3):
-            v = jnp.where(halo, roll(arrived, -4 * f), g[s, f])
-            tip = jnp.where(beyond_rows & in_y, sg[f], v[24:32])
-            v = jnp.concatenate([v[0:24], tip], axis=0)
-            state.append(jnp.where(first, v, 0.0))
-        state = edge_substep(state, jnp.where(first, k, 0.0), k, q, SPAN)
+            ahead = {}
+            for i in range(-reach[f], reach[f] + 1):
+                v = jnp.where(((part_t + i - 4 * s) & 15) < 4, roll(arrived, -4 * f - i), pre[f, i + 2])
+                tip = jnp.where(beyond_rows & (mask[s, 2, i + 2, 0:8] > 0.5), sg[f, i + 2], v[24:32])
+                v = jnp.concatenate([v[0:24], tip], axis=0)
+                ahead[i] = jnp.where(mask[s, 0, i + 2] > 0.5, v, 0.0)
+            state.append(ahead)
+        state = edge_substep(*state, {i: k * mask[s, 0, i + 2] for i in (-1, 0, 1)}, k, q, SPAN)
+        second = mask[s, 1, 2] > 0.5
         laid = []
         for f in range(3):
             v = state[f]
-            low = jnp.where((sub < 3) & own_low, sg[f], v[0:8])
-            high = jnp.where((sub >= 5) & own_high, sg[f], v[16:24])
+            low = jnp.where((sub < 3) & own_low, sg[f, 2], v[0:8])
+            high = jnp.where((sub >= 5) & own_high, sg[f, 2], v[16:24])
             v = jnp.concatenate([low, v[8:16], high, v[24:32]], axis=0)
             v = jnp.where(own_strip, nso[f], v)
-            laid.append(jnp.where(second, v, 0.0))
-        return edge_substep(laid, jnp.where(second, k, 0.0), k, q, ROWS)
+            v = jnp.where(second, v, 0.0)
+            near = v if f == 0 else v[0:ROWS]
+            ahead = {0: v, 1: roll(near, -1), -1: roll(near, 1)}
+            if f == 0:
+                ahead[2], ahead[-2] = roll(v[0:ROWS], -2), roll(v[0:ROWS], 2)
+            laid.append(ahead)
+        return edge_substep(*laid, {i: k * mask[s, 1, i + 2] for i in (-1, 0, 1)}, k, q, ROWS)
 
     @pl.when(at_upper)
     def _():
@@ -710,8 +741,10 @@
     def _():
         wait_recv(y_sends[1])
 
+    edge_before(side)
     for f, v in enumerate(edge_side(side)):
         done[f] = v
+    edge_before(1 - side)
 
     for a, dx in enumerate((-1, 1)):
         x_wait(sent.at[a], has(dx, 0))
@@ -721,9 +754,12 @@
         def _(c=c):
             c.wait_send()
 
-    @pl.when(both(at_lower, has_mate))
+    @pl.when(both(at_lower, last_column))
     def _():
         first_hop.wait_send()
+
+    @pl.when(both(at_lower, beside_last))
+    def _():
         last_hop.wait_send()
 
     @pl.when(both(at_lower, seam_west))
@@ -792,12 +828,13 @@
             vmem((2, 2) + TILE, F32),
             vmem((3, 3, LEVELS, WIDE), F32),
             vmem((3, 8) + TILE, F32),
-            vmem((3,) + TILE, F32),
+            vmem((3, 5) + TILE, F32),
             vmem((2, 3) + TILE, F32),
             vmem((3, SPAN) + TILE, F32),
             vmem((3, SPAN, LANES), F32),
             vmem((2,) + TILE, F32),
-            vmem((2, 3, SPAN, LANES), F32),
+            vmem((3, 5, SPAN, LANES), F32),
+            vmem((2, 3, 5, SPAN, LANES), F32),
             vmem((2, 2) + TILE, F32),
             vmem((3, ROWS, LANES), F32),
             vmem((96, LANES), F32),

time: 12.5 us -> 12.4 us (level)
  the two profiles are of different devices: /device:TPU:224 before, /device:TPU:27 now
where the time goes in v6:
time: 12.4 us; the launch traced here: 12.2 us
  Pallas kernels  12.2 us (98%)
    pallas_call x1, Pallas kernels, body(): pl.pallas_call(functools.partial(exchange_kernel, sizes), out_shape=vmem(...  11.3 us
    pallas_call x1, Pallas kernels, body(): pl.pallas_call(write_kernel, out_shape=jax.ShapeDtypeStruct(fields.shape,...  0.92 us

profile of v6, /device:TPU:27, one launch (start us, length us, event | category | flops | bytes accessed | tf_op | source)
XLA Modules:
  0.0 12.2 jit_solution(16082684886036781962)
XLA Ops:
  0.0 11.3 %shard_map.100.ready = f32[3,3,8,24,128]{4,3,2,1,0:T(8,128)S(1)} custom-call(f32[3,8,24,384]{3,2,1,0:T(8,128)} %fields.1, f32[96,128]{1,0:T(8,128)} %bitcast.2, f32[96,8]{1,0:T(8,128)} %bitcast.3, s32[2,384]{1,0:T(2,128)} %east_index.1, s32[2,24]{1,0:T(2,128)} %north_index.1, f32[2,384]{1,0:T(2,128)} %east_weight.1, f32[2,24]{1,0:T(2,128)} %north_weight.1, ...), custom_call_target="tpu_custom_call" | custom-call | tf_op jit(solution)/shard_map/pallas_call | solution.py:813
  11.3 0.9 %shard_map.101 = f32[3,8,24,384]{3,2,1,0:T(8,128)} custom-call(f32[3,3,8,24,128]{4,3,2,1,0:T(8,128)S(1)} %shard_map.100.ready), custom_call_target="tpu_custom_call" | custom-call | tf_op jit(solution)/shard_map/pallas_call | solution.py:870

commit v7 on v6

--- a/solution.py
+++ b/solution.py
@@ -791,7 +791,10 @@
 
 def write_kernel(ready, out, sem):
     for j in range(3):
-        pltpu.make_async_copy(ready.at[j], out.at[:, :, :, LANES * j : LANES * j + LANES], sem).start()
+        for f in range(3):
+            for l in range(LEVELS):
+                cut = slice(LANES * j, LANES * j + LANES)
+                pltpu.make_async_copy(ready.at[j, f, l], out.at[f, l, :, cut], sem).start()
     pltpu.make_async_copy(ready, ready, sem).wait()
 
 

time: 12.4 us -> 12.3 us (level)
  no operation moved by 1% of the time
where the time goes in v7:
time: 12.3 us; the launch traced here: 12.1 us
  Pallas kernels  12.1 us (98%)
    pallas_call x1, Pallas kernels, body(): pl.pallas_call(functools.partial(exchange_kernel, sizes), out_shape=vmem(...  11.3 us
    pallas_call x1, Pallas kernels, body(): pl.pallas_call(write_kernel, out_shape=jax.ShapeDtypeStruct(fields.shape,...  0.87 us

profile of v7, /device:TPU:27, one launch (start us, length us, event | category | flops | bytes accessed | tf_op | source)
XLA Modules:
  0.0 12.1 jit_solution(274204095037534353)
XLA Ops:
  0.0 11.3 %shard_map.100.ready = f32[3,3,8,24,128]{4,3,2,1,0:T(8,128)S(1)} custom-call(f32[3,8,24,384]{3,2,1,0:T(8,128)} %fields.1, f32[96,128]{1,0:T(8,128)} %bitcast.2, f32[96,8]{1,0:T(8,128)} %bitcast.3, s32[2,384]{1,0:T(2,128)} %east_index.1, s32[2,24]{1,0:T(2,128)} %north_index.1, f32[2,384]{1,0:T(2,128)} %east_weight.1, f32[2,24]{1,0:T(2,128)} %north_weight.1, ...), custom_call_target="tpu_custom_call" | custom-call | tf_op jit(solution)/shard_map/pallas_call | solution.py:816
  11.3 0.9 %shard_map.101 = f32[3,8,24,384]{3,2,1,0:T(8,128)} custom-call(f32[3,3,8,24,128]{4,3,2,1,0:T(8,128)S(1)} %shard_map.100.ready), custom_call_target="tpu_custom_call" | custom-call | tf_op jit(solution)/shard_map/pallas_call | solution.py:873

commit v8 on v7

--- a/solution.py
+++ b/solution.py
@@ -366,8 +366,8 @@
     last_hop = to(
         0, 1, hop.at[0], from_d.at[1 - east_one, 0], sent.at[8], received.at[4 + 2 * (1 - east_one)]
     )
-    first_seam_hop = to(-1, 0, to_y.at[1, 0], hop.at[1], sent.at[5], received.at[9])
-    last_seam_hop = to(0, 1, hop.at[1], from_d.at[1, 0], sent.at[9], received.at[6])
+    first_seam_hop = to(-1, 0, to_y.at[1, 0], hop.at[0], sent.at[5], received.at[8])
+    last_seam_hop = to(0, 1, hop.at[0], from_d.at[1, 0], sent.at[5], received.at[6])
 
     def start(group, extra=None):
         for there, c, _ in group:
@@ -835,7 +835,7 @@
             vmem((2, 3) + TILE, F32),
             vmem((3, SPAN) + TILE, F32),
             vmem((3, SPAN, LANES), F32),
-            vmem((2,) + TILE, F32),
+            vmem((1,) + TILE, F32),
             vmem((3, 5, SPAN, LANES), F32),
             vmem((2, 3, 5, SPAN, LANES), F32),
             vmem((2, 2) + TILE, F32),
@@ -851,8 +851,8 @@
             pltpu.SMEM((2, 2), I32),
             pltpu.SMEM((LEVELS,), F32),
             pltpu.SMEM((LEVELS,), F32),
-            dma((10,)),
-            dma((10,)),
+            dma((9,)),
+            dma((9,)),
             pltpu.SemaphoreType.REGULAR,
         ],
         compiler_params=pltpu.CompilerParams(

time: 12.3 us -> 12.3 us (level)
  no operation moved by 1% of the time
where the time goes in v8:
time: 12.3 us; the launch traced here: 12.1 us
  Pallas kernels  12.1 us (98%)
    pallas_call x1, Pallas kernels, body(): pl.pallas_call(functools.partial(exchange_kernel, sizes), out_shape=vmem(...  11.2 us
    pallas_call x1, Pallas kernels, body(): pl.pallas_call(write_kernel, out_shape=jax.ShapeDtypeStruct(fields.shape,...  0.87 us

profile of v8, /device:TPU:27, one launch (start us, length us, event | category | flops | bytes accessed | tf_op | source)
XLA Modules:
  0.0 12.1 jit_solution(1499283074742299348)
XLA Ops:
  0.0 11.2 %shard_map.100.ready = f32[3,3,8,24,128]{4,3,2,1,0:T(8,128)S(1)} custom-call(f32[3,8,24,384]{3,2,1,0:T(8,128)} %fields.1, f32[96,128]{1,0:T(8,128)} %bitcast.2, f32[96,8]{1,0:T(8,128)} %bitcast.3, s32[2,384]{1,0:T(2,128)} %east_index.1, s32[2,24]{1,0:T(2,128)} %north_index.1, f32[2,384]{1,0:T(2,128)} %east_weight.1, f32[2,24]{1,0:T(2,128)} %north_weight.1, ...), custom_call_target="tpu_custom_call" | custom-call | tf_op jit(solution)/shard_map/pallas_call | solution.py:816
  11.2 0.9 %shard_map.101 = f32[3,8,24,384]{3,2,1,0:T(8,128)} custom-call(f32[3,3,8,24,128]{4,3,2,1,0:T(8,128)S(1)} %shard_map.100.ready), custom_call_target="tpu_custom_call" | custom-call | tf_op jit(solution)/shard_map/pallas_call | solution.py:873

commit v9 on v8

--- a/solution.py
+++ b/solution.py
@@ -790,9 +790,9 @@
 
 
 def write_kernel(ready, out, sem):
-    for j in range(3):
-        for f in range(3):
-            for l in range(LEVELS):
+    for f in range(3):
+        for l in range(LEVELS):
+            for j in range(3):
                 cut = slice(LANES * j, LANES * j + LANES)
                 pltpu.make_async_copy(ready.at[j, f, l], out.at[f, l, :, cut], sem).start()
     pltpu.make_async_copy(ready, ready, sem).wait()

time: 12.3 us -> 12.3 us (level)
  no operation moved by 1% of the time
where the time goes in v9:
time: 12.3 us; the launch traced here: 12.1 us
  Pallas kernels  12.1 us (98%)
    pallas_call x1, Pallas kernels, body(): pl.pallas_call(functools.partial(exchange_kernel, sizes), out_shape=vmem(...  11.2 us
    pallas_call x1, Pallas kernels, body(): pl.pallas_call(write_kernel, out_shape=jax.ShapeDtypeStruct(fields.shape,...  0.87 us

profile of v9, /device:TPU:27, one launch (start us, length us, event | category | flops | bytes accessed | tf_op | source)
XLA Modules:
  0.0 12.1 jit_solution(3377135294148984893)
XLA Ops:
  0.0 11.2 %shard_map.100.ready = f32[3,3,8,24,128]{4,3,2,1,0:T(8,128)S(1)} custom-call(f32[3,8,24,384]{3,2,1,0:T(8,128)} %fields.1, f32[96,128]{1,0:T(8,128)} %bitcast.2, f32[96,8]{1,0:T(8,128)} %bitcast.3, s32[2,384]{1,0:T(2,128)} %east_index.1, s32[2,24]{1,0:T(2,128)} %north_index.1, f32[2,384]{1,0:T(2,128)} %east_weight.1, f32[2,24]{1,0:T(2,128)} %north_weight.1, ...), custom_call_target="tpu_custom_call" | custom-call | tf_op jit(solution)/shard_map/pallas_call | solution.py:816
  11.2 0.9 %shard_map.101 = f32[3,8,24,384]{3,2,1,0:T(8,128)} custom-call(f32[3,3,8,24,128]{4,3,2,1,0:T(8,128)S(1)} %shard_map.100.ready), custom_call_target="tpu_custom_call" | custom-call | tf_op jit(solution)/shard_map/pallas_call | solution.py:873
